TPU v7x, 128 devices: a whole 4x4x4 slice. The times are simulated.
128 devices in a mesh: dp: 8 (over y, x_hi), tensor: 16 (over z, x_lo, core).
Axes of the slice: x: 4 (x_hi: 2, x_lo: 2; x = x_hi * 2 + x_lo), y: 4, z: 4, core: 2. Of those that a mesh axis runs over, the one named last changes fastest.
Arguments:
- grad: bfloat16 [4096, 4096], P(('dp', 'tensor')), may hold values from -6 to 6
- left_basis: float32 [4096, 4096], P('dp', 'tensor'), may hold values from -0.09375 to 0.09375
- right_basis: float32 [4096, 4096], P('dp', 'tensor'), may hold values from -0.09375 to 0.09375
- first_moment: float32 [4096, 4096], P('dp', 'tensor'), may hold values from -3 to 3
- second_moment: float32 [4096, 4096], P('dp', 'tensor'), may hold values from 0.1 to 10
Outputs:
- update: float32 [4096, 4096], P(('dp', 'tensor'))
- new_first: float32 [4096, 4096], P('dp', 'tensor')
- new_second: float32 [4096, 4096], P('dp', 'tensor')
All inputs are finite; a program needn't handle non-finite values.
Results may differ from a plain program's by a relative error of at most 0.0003.
Values may be sent and summed in bfloat16 or wider, within the bound.
A program may use at most 128 MiB of HBM per device.

v0:
```python
import jax
import jax.numpy as jnp
from jax import lax
from jax.sharding import PartitionSpec as P

STEP = 10


def body(grad, left_basis, right_basis, first_moment, second_moment):
    highest = lax.Precision.HIGHEST
    blocked = lax.all_to_all(grad, "tensor", split_axis=1, concat_axis=0, tiled=True)
    partial_left = jnp.einsum(
        "rc,rk->ck",
        lax.all_gather(blocked, "tensor", axis=1, tiled=True).astype(jnp.float32),
        left_basis,
        precision=highest,
        preferred_element_type=jnp.float32,
    )
    half_turned = lax.psum_scatter(partial_left, "dp", scatter_dimension=0, tiled=True)
    partial_right = jnp.einsum(
        "ci,cj->ij",
        lax.all_gather(half_turned, "tensor", axis=1, tiled=True),
        right_basis,
        precision=highest,
        preferred_element_type=jnp.float32,
    )
    rotated = lax.psum_scatter(partial_right, "dp", scatter_dimension=0, tiled=True)
    new_first = 0.9 * first_moment + 0.1 * rotated
    new_second = 0.95 * second_moment + 0.05 * rotated * rotated
    first_fix = 1.0 - 0.9**STEP
    second_fix = 1.0 - 0.95**STEP
    direction = new_first / first_fix / (jnp.sqrt(new_second / second_fix) + 1e-08)
    partial_back = jnp.einsum(
        "cj,ij->ci",
        right_basis,
        lax.all_gather(direction, "dp", axis=0, tiled=True),
        precision=highest,
        preferred_element_type=jnp.float32,
    )
    half_back = lax.psum_scatter(partial_back, "tensor", scatter_dimension=1, tiled=True)
    gathered = lax.all_gather(half_back, "dp", axis=0, tiled=True)
    partial_update = jnp.einsum(
        "ri,ci->rc", left_basis, gathered, precision=highest, preferred_element_type=jnp.float32
    )
    summed = lax.psum_scatter(partial_update, "tensor", scatter_dimension=1, tiled=True)
    update = lax.all_to_all(summed, "tensor", split_axis=0, concat_axis=1, tiled=True)
    return (update, new_first, new_second)


def solution(mesh):
    placed = (
        P(("dp", "tensor"), None),
        P("dp", "tensor"),
        P("dp", "tensor"),
        P("dp", "tensor"),
        P("dp", "tensor"),
    )
    return jax.shard_map(
        body,
        mesh=mesh,
        in_specs=placed,
        out_specs=(P(("dp", "tensor"), None), P("dp", "tensor"), P("dp", "tensor")),
        check_vma=False,
    )
```

profile of v0, /device:TPU:1, one launch (start us, length us, event | category | flops | bytes accessed | tf_op | source)
XLA Modules:
  0.0 703.7 jit_solution(10487702188994949333)
XLA Ops:
  7.2 0.0 copy-start
  7.2 0.0 all-gather.5.cloned.1.call-start
  7.2 1.0 copy.19
  8.2 14.8 %all_to_all.38 = bf16[32,16,256]{2,0,1:T(8,128)(2,1)} all-to-all(bf16[32,16,256]{2,0,1:T(8,128)(2,1)S(1)} %bitcast.26), channel_id=1, replica_groups=mesh['dp'=8,'tensor'=16] {'tensor'}, dimensions={1} | all-to-all | bytes 524288 | tf_op jit(solution)/shard_map/all_to_all | solution.py:11
  23.1 0.0 all-gather.5.cloned.1.call-update
  23.1 0.0 reduce-scatter.5.cloned.1.call-start
  23.2 45.2 %all-gather.5.cloned.1.call-done = bf16[512,4096]{1,0:T(8,128)(2,1)} async-done(((bf16[512,256]{1,0:T(8,128)(2,1)}), bf16[512,4096]{1,0:T(8,128)(2,1)}) %all-gather.5.cloned.1.call-update) | async-done | bytes 4194320 | tf_op jit(solution)/shard_map/all_gather | solution.py:14
  68.4 8.9 %fusion.2 = f32[4096,256]{1,0:T(8,128)} fusion(bf16[512,4096]{1,0:T(8,128)(2,1)} %all-gather.5.cloned.1.call-done, f32[512,256]{1,0:T(8,128)} %param.6), kind=kOutput, calls=%fused_computation.7 | convolution fusion | flops 6442450944 | bytes 8912896 | tf_op jit(solution)/shard_map/rc,rk->ck/dot_general | solution.py:12
  77.3 0.0 reduce-scatter.5.cloned.1.call-update
  77.3 0.0 all-gather.7.cloned.1.call-start
  77.4 83.0 %reduce-scatter.5.cloned.1.call-done = f32[512,256]{1,0:T(8,128)} async-done(((f32[4096,256]{1,0:T(8,128)}), f32[512,256]{1,0:T(8,128)}) %reduce-scatter.5.cloned.1.call-update) | async-done | bytes 524304 | tf_op jit(solution)/shard_map/reduce_scatter | solution.py:19
  160.4 0.0 all-gather.7.cloned.1.call-update
  160.4 0.2 reduce-scatter.7.cloned.1.call-start
  160.7 54.0 %all-gather.7.cloned.1.call-done = f32[512,4096]{1,0:T(8,128)} async-done(((f32[512,256]{1,0:T(8,128)}), f32[512,4096]{1,0:T(8,128)}) %all-gather.7.cloned.1.call-update) | async-done | bytes 8388624 | tf_op jit(solution)/shard_map/all_gather | solution.py:22
  214.7 0.0 copy-done
  214.7 16.9 %fusion.3 = f32[4096,256]{1,0:T(8,128)} fusion(f32[512,4096]{1,0:T(8,128)} %all-gather.7.cloned.1.call-done, f32[512,256]{1,0:T(8,128)S(1)} %copy-done), kind=kOutput, calls=%fused_computation.8 | convolution fusion | flops 6442450944 | bytes 13107200 | tf_op jit(solution)/shard_map/ci,cj->ij/dot_general | solution.py:20
  231.6 0.0 copy-start.2
  231.6 0.0 copy-start.3
  231.6 0.0 reduce-scatter.7.cloned.1.call-update
  231.7 0.0 all-gather.9.cloned.1.call-start
  231.7 84.2 %reduce-scatter.7.cloned.1.call-done = f32[512,256]{1,0:T(8,128)} async-done(((f32[4096,256]{1,0:T(8,128)}), f32[512,256]{1,0:T(8,128)}) %reduce-scatter.7.cloned.1.call-update) | async-done | bytes 524304 | tf_op jit(solution)/shard_map/reduce_scatter | solution.py:27
  315.9 0.0 copy-done.2
  315.9 0.0 copy-done.3
  315.9 2.4 add_divide_fusion
  318.2 0.0 all-gather.9.cloned.1.call-update
  318.2 0.0 reduce-scatter.9.cloned.1.call-start
  318.3 71.1 %all-gather.9.cloned.1.call-done = f32[4096,256]{1,0:T(8,128)} async-done(((f32[512,256]{1,0:T(8,128)}), f32[4096,256]{1,0:T(8,128)}) %all-gather.9.cloned.1.call-update) | async-done | bytes 4194320 | tf_op jit(solution)/shard_map/all_gather | solution.py:36
  389.4 10.7 %convolution_bitcast_fusion.1 = f32[512,4096]{0,1:T(8,128)} fusion(f32[4096,256]{1,0:T(8,128)} %all-gather.9.cloned.1.call-done, f32[512,256]{1,0:T(8,128)S(1)} %copy-done), kind=kOutput, calls=%fused_computation.1 | convolution fusion | flops 6442450944 | bytes 13107200 | tf_op jit(solution)/shard_map/cj,ij->ci/dot_general | solution.py:33
  400.0 0.0 copy-start.1
  400.0 0.0 reduce-scatter.9.cloned.1.call-update
  400.0 0.0 all-gather.11.cloned.1.call-start
  400.1 94.5 %reduce-scatter.9.cloned.1.call-done = f32[512,256]{0,1:T(8,128)} async-done(((f32[512,4096]{0,1:T(8,128)}), f32[512,256]{0,1:T(8,128)}) %reduce-scatter.9.cloned.1.call-update) | async-done | bytes 524304 | tf_op jit(solution)/shard_map/reduce_scatter | solution.py:40
  494.6 0.0 all-gather.11.cloned.1.call-update
  494.6 0.3 reduce-scatter.11.cloned.1.call-start
  494.9 73.4 %all-gather.11.cloned.1.call-done = f32[4096,256]{0,1:T(8,128)} async-done(((f32[512,256]{0,1:T(8,128)}), f32[4096,256]{0,1:T(8,128)}) %all-gather.11.cloned.1.call-update) | async-done | bytes 4194320 | tf_op jit(solution)/shard_map/all_gather | solution.py:41
  568.3 0.0 copy-done.1
  568.3 17.0 %convolution_bitcast_fusion = f32[512,4096]{0,1:T(8,128)} fusion(f32[4096,256]{0,1:T(8,128)} %all-gather.11.cloned.1.call-done, f32[512,256]{1,0:T(8,128)S(1)} %copy-done.1), kind=kOutput, calls=%fused_computation | convolution fusion | flops 6442450944 | bytes 13107200 | tf_op jit(solution)/shard_map/ri,ci->rc/dot_general | solution.py:42
  585.3 0.0 reduce-scatter.11.cloned.1.call-update
  585.3 94.6 %reduce-scatter.11.cloned.1.call-done = f32[512,256]{0,1:T(8,128)} async-done(((f32[512,4096]{0,1:T(8,128)}), f32[512,256]{0,1:T(8,128)}) %reduce-scatter.11.cloned.1.call-update) | async-done | bytes 524304 | tf_op jit(solution)/shard_map/reduce_scatter | solution.py:45
  679.9 1.2 copy.14
  681.1 14.9 %all_to_all.39 = f32[16,32,256]{2,1,0:T(8,128)S(1)} all-to-all(f32[16,32,256]{2,1,0:T(8,128)S(1)} %bitcast.23), channel_id=1, replica_groups=mesh['dp'=8,'tensor'=16] {'tensor'}, dimensions={0} | all-to-all | bytes 1048576 | tf_op jit(solution)/shard_map/all_to_all | solution.py:46
  696.0 0.8 copy.17
Async XLA Ops:
  7.2 207.5 %copy-start = (f32[512,256]{1,0:T(8,128)S(1)}, f32[512,256]{1,0:T(8,128)}, u32[]{:S(2)}) copy-start(f32[512,256]{1,0:T(8,128)} %param.7) | copy-start | bytes 1572868
  7.2 61.2 %all-gather.5.cloned.1.call-start = ((), (), s32[]{:S(2)}) async-start(), calls=%async_computation.6 | async-start | bytes 4456448 | tf_op jit(solution)/shard_map/all_gather | solution.py:14
  23.1 137.3 %reduce-scatter.5.cloned.1.call-start = ((), (), s32[]{:S(2)}) async-start(), calls=%async_computation.7 | async-start | bytes 4718592 | tf_op jit(solution)/shard_map/reduce_scatter | solution.py:19
  77.3 137.4 %all-gather.7.cloned.1.call-start = ((), (), s32[]{:S(2)}) async-start(), calls=%async_computation.8 | async-start | bytes 8912896 | tf_op jit(solution)/shard_map/all_gather | solution.py:22
  160.4 155.4 %reduce-scatter.7.cloned.1.call-start = ((), (), s32[]{:S(2)}) async-start(), calls=%async_computation.9 | async-start | bytes 4718592 | tf_op jit(solution)/shard_map/reduce_scatter | solution.py:27
  231.6 84.2 %copy-start.2 = (f32[512,256]{1,0:T(8,128)S(1)}, f32[512,256]{1,0:T(8,128)}, u32[]{:S(2)}) copy-start(f32[512,256]{1,0:T(8,128)} %param.8) | copy-start | bytes 1572868
  231.6 84.2 %copy-start.3 = (f32[512,256]{1,0:T(8,128)S(1)}, f32[512,256]{1,0:T(8,128)}, u32[]{:S(2)}) copy-start(f32[512,256]{1,0:T(8,128)} %param.9) | copy-start | bytes 1572868
  231.7 157.7 %all-gather.9.cloned.1.call-start = ((), (), s32[]{:S(2)}) async-start(), calls=%async_computation.10 | async-start | bytes 4718592 | tf_op jit(solution)/shard_map/all_gather | solution.py:36
  318.2 176.4 %reduce-scatter.9.cloned.1.call-start = ((), (), s32[]{:S(2)}) async-start(), calls=%async_computation.11 | async-start | bytes 8912896 | tf_op jit(solution)/shard_map/reduce_scatter | solution.py:40
  400.0 168.3 %copy-start.1 = (f32[512,256]{1,0:T(8,128)S(1)}, f32[512,256]{1,0:T(8,128)}, u32[]{:S(2)}) copy-start(f32[512,256]{1,0:T(8,128)} %param.6) | copy-start | bytes 1572868
  400.0 168.3 %all-gather.11.cloned.1.call-start = ((), (), s32[]{:S(2)}) async-start(), calls=%async_computation.12 | async-start | bytes 4718592 | tf_op jit(solution)/shard_map/all_gather | solution.py:41
  494.6 185.2 %reduce-scatter.11.cloned.1.call-start = ((), (), s32[]{:S(2)}) async-start(), calls=%async_computation.13 | async-start | bytes 8912896 | tf_op jit(solution)/shard_map/reduce_scatter | solution.py:45
Sparse Core Ops, SparseCore 0:
  23.2 45.0 all-gather.4
  77.5 82.9 reduce-scatter.4
  162.2 52.4 all-gather.6
  231.8 84.0 reduce-scatter.6
  318.6 70.6 all-gather.8
  400.2 94.4 reduce-scatter.8
  496.9 71.3 all-gather.10
  585.4 94.4 reduce-scatter.10
where the time goes:
time: 704 us
  waiting for transfers between devices  600 us (85%)
  matrix products  53.5 us (8%)
  blocking collectives  29.7 us (4%)
  between operations  14.2 us (2%)
    reduce_scatter x1, waiting for transfers between devices, body(): lax.psum_scatter(partial_update, 'tensor', scatter_dimension=1, tiled=True)  94.6 us
    reduce_scatter x1, waiting for transfers between devices, body(): lax.psum_scatter(partial_back, 'tensor', scatter_dimension=1, tiled=True)  94.5 us
    reduce_scatter x1, waiting for transfers between devices, body(): lax.psum_scatter(partial_right, 'dp', scatter_dimension=0, tiled=True)  84.2 us
    reduce_scatter x1, waiting for transfers between devices, body(): lax.psum_scatter(partial_left, 'dp', scatter_dimension=0, tiled=True)  83 us
    all_gather x1, waiting for transfers between devices, body(): gathered = lax.all_gather(half_back, 'dp', axis=0, tiled=True)  73.4 us
    all_gather x1, waiting for transfers between devices, body(): lax.all_gather(direction, 'dp', axis=0, tiled=True)  71.1 us
    all_gather x1, waiting for transfers between devices, body(): lax.all_gather(half_turned, 'tensor', axis=1, tiled=True)  54 us
    all_gather x1, waiting for transfers between devices, body(): lax.all_gather(blocked, 'tensor', axis=1, tiled=True).astype(jnp.float32)  45.2 us
  transfers between devices with their start and end apart: 8, of which 8 were waited for; matrix products, arithmetic and copies ran while one was open for 0% of the time, Pallas kernels for 0%

commit v1 on v0

v1 whole, which is shorter than its diff:
```python
import functools

import jax
import jax.numpy as jnp
from jax import lax
from jax.experimental import pallas as pl
from jax.experimental.pallas import tpu as pltpu
from jax.sharding import PartitionSpec as P

STEP = 10
F32 = jnp.float32
BF16 = jnp.bfloat16
MESH = pl.DeviceIdType.MESH

SPAN = 250.0
BASE = 124.0
BOUND = 0.09375


def encode(x, inverse):
    t = jnp.maximum(jnp.abs(x) * inverse, 1e-30)
    y = jnp.exp2((t * lax.rsqrt(t)) * SPAN - BASE)
    return jnp.where(x < 0, -y, y).astype(BF16)


def decode(code, scale):
    y = code.astype(F32)
    t = (jnp.log2(jnp.abs(y)) + BASE) * (1.0 / SPAN)
    v = t * t * scale
    return jnp.where(y < 0, -v, v)


def pack(get, message, rows, blocks):
    most = None
    for b in range(blocks):
        a = jnp.abs(get(b))
        most = a if most is None else jnp.maximum(most, a)
    most = jnp.max(jnp.max(most, axis=0, keepdims=True), axis=1, keepdims=True)
    scale16 = (jnp.broadcast_to(most, (16, 128)) * 1.01 + 1e-30).astype(BF16)
    message[pl.ds(blocks * rows, 16), :] = scale16
    inverse = 1.0 / scale16.astype(F32)[0:1, :]
    for b in range(blocks):
        message[pl.ds(b * rows, rows), :] = encode(get(b), inverse)


def unpack(message, b, rows, blocks):
    scale = message[pl.ds(blocks * rows, 16), :].astype(F32)[0:1, :]
    return decode(message[pl.ds(b * rows, rows), :], scale)


def halves(x):
    hi = x.astype(BF16)
    return hi, (x - hi.astype(F32)).astype(BF16)


def dot(a, b):
    return lax.dot_general(a, b, (((1,), (0,)), ((), ())), preferred_element_type=F32)


def dot_t(a, b):
    return lax.dot_general(a, b, (((1,), (1,)), ((), ())), preferred_element_type=F32)


def kernel(
    grad, left, right, first, second, update, new_first, new_second,
    left_out, left_in, lt, lf, grad_out, grad_in, right_out, right_in, right_hi, right_lo,
    h_out, h_in, h_gather_out, h_gather_in, h_block, h_parts,
    rot_out, rot_in, d_out, d_in, d_parts, y_block, y_out, y_in, y_gather_out, y_gather_in, y_hi, y_lo,
    u_block, u_out, u_in, u_last_out, u_last_in,
    ss, rs,
):
    dp = lax.axis_index("dp")
    tensor = lax.axis_index("tensor")
    y, xh = dp // 2, dp % 2
    z, xl, core = tensor // 4, (tensor // 2) % 2, tensor % 2
    x = xh * 2 + xl
    other = 1 - core

    def device(px, py, pz, pc):
        return (py * 2 + px // 2, pz * 4 + (px % 2) * 2 + pc)

    def turn(a, o):
        return (a + o) % 4

    sems = {}
    total = [0, 0]

    def bank(name, sends, receives):
        sems[name] = tuple(total)
        total[0] += sends
        total[1] += receives

    for name, sends, receives in (
        ("l1", 4, 4), ("lg", 4, 4), ("lc", 4, 4), ("g1", 8, 8), ("g2", 4, 4),
        ("r1", 4, 4), ("rg", 4, 4), ("rc", 4, 4), ("h1", 8, 8), ("h2", 4, 4),
        ("p", 16, 16), ("d", 16, 16), ("y1", 4, 4), ("y2", 8, 8), ("u1", 4, 4), ("u2", 8, 8),
    ):
        bank(name, sends, receives)

    pending = []

    def remote(name, i, j, src, dst, target):
        return pltpu.make_async_remote_copy(
            src_ref=src, dst_ref=dst, send_sem=ss.at[sems[name][0] + i], recv_sem=rs.at[sems[name][1] + j],
            device_id=device(*target), device_id_type=MESH,
        )

    def send(name, i, j, src, dst, target):
        copy = remote(name, i, j, src, dst, target)
        copy.start()
        pending.append(copy.wait_send)

    def send_unless(own, name, i, j, src, dst, target):
        here = pltpu.make_async_copy(src, dst, rs.at[sems[name][1] + j])
        there = remote(name, i, j, src, dst, target)
        pl.when(own)(here.start)
        pl.when(jnp.logical_not(own))(there.start)
        pending.append(lambda: pl.when(jnp.logical_not(own))(there.wait_send))

    def arrive(name, j, dst):
        pltpu.make_async_copy(dst, dst, rs.at[sems[name][1] + j]).wait()

    barrier = pltpu.get_barrier_semaphore()
    peers = [(x, turn(y, a), turn(z, b), core) for a in range(4) for b in range(4) if a or b]
    peers += [(turn(x, o), y, z, c) for o in range(4) for c in (core, other) if o or c is other]
    peers += [(x, y, turn(z, o), other) for o in (1, 2, 3)]
    for peer in peers:
        pl.semaphore_signal(barrier, inc=1, device_id=device(*peer), device_id_type=MESH)

    for b in range(4):
        left_out[b] = encode(left[pl.ds(b * 128, 128), :].T, 1.0 / BOUND)
    for px in range(4):
        for pc in range(2):
            for b in range(4):
                grad_out[px, pc, :, pl.ds(b * 128, 128)] = grad[:, pl.ds(pc * 2048 + b * 512 + px * 128, 128)]

    pl.semaphore_wait(barrier, len(peers))

    for o in (2, 1, 3, 0):
        to = turn(z, o)
        args = ("l1", o, y, left_out.at[to], left_in.at[x, core, y], (x, z, to, core))
        if o:
            send(*args)
        else:
            send_unless(y == z, *args)

    own_rows = pl.ds(pl.multiple_of(y * 256 + x * 64 + core * 32, 32), 32)
    for o in (2, 1, 3, 0):
        for oc, pc in ((1, other), (0, core)):
            if o or oc:
                px = turn(x, o)
                send("g1", o * 2 + oc, o * 2 + oc, grad_out.at[px, pc], grad_in.at[own_rows], (px, y, z, pc))
    grad_in[own_rows] = grad_out[x, core]

    for q in range(4):
        for b in range(2):
            right_out[q, pl.ds(b * 128, 128), :] = encode(
                right[pl.ds(q * 128, 128), pl.ds(b * 128, 128)], 1.0 / BOUND
            )
    for o in (2, 1, 3):
        px = turn(x, o)
        send("r1", o, o, right_out.at[px], right_in.at[y, core, x], (px, y, z, core))
    right_in[y, core, x] = right_out[x]

    for i in range(4):
        arrive("l1", i, left_in.at[x, core, i])
    for o in (2, 1, 3):
        piece = left_in.at[x, core]
        send("lg", o, o, piece, piece, (turn(x, o), y, z, core))
    send("lc", 0, 0, left_in.at[x, core], left_in.at[x, core], (x, y, z, other))

    for o in range(4):
        for oc, pc in ((1, other), (0, core)):
            if o or oc:
                px = turn(x, 4 - o)
                rows = pl.ds(pl.multiple_of(y * 256 + px * 64 + pc * 32, 32), 32)
                arrive("g1", o * 2 + oc, grad_in.at[rows])
    own_rows = pl.ds(pl.multiple_of(y * 256, 256), 256)
    for o in (2, 1, 3):
        send("g2", o, o, grad_in.at[own_rows], grad_in.at[own_rows], (x, turn(y, o), z, core))

    for o in (1, 2, 3):
        arrive("r1", o, right_in.at[y, core, turn(x, 4 - o)])
    for o in (2, 1, 3):
        piece = right_in.at[y, core]
        send("rg", o, o, piece, piece, (x, turn(y, o), z, core))
    send("rc", 0, 0, right_in.at[y, core], right_in.at[y, core], (x, y, z, other))

    def left_piece(px, pc):
        def one(ry, carry):
            for h in range(2):
                v = decode(left_in[px, pc, ry, pl.ds(h * 128, 128), :], BOUND)
                hi, lo = halves(v)
                chunk = (px % 2) * 4 + pc * 2 + h
                at = pl.ds(pl.multiple_of(ry * 256 + (px // 2) * 128, 128), 128)
                lt[chunk, pl.ds(0, 128), at] = hi
                lt[chunk, pl.ds(128, 128), at] = lo
            return carry

        lax.fori_loop(0, 4, one, 0)

    left_piece(x, core)
    for o in (1, 3, 2):
        px = turn(x, 4 - o)
        arrive("lg", o, left_in.at[px, core])
        send("lc", o, o, left_in.at[px, core], left_in.at[px, core], (x, y, z, other))
        left_piece(px, core)
    for o in (0, 1, 3, 2):
        px = turn(x, 4 - o)
        arrive("lc", o, left_in.at[px, other])
        left_piece(px, other)

    for o in (1, 2, 3):
        rows = pl.ds(pl.multiple_of(turn(y, 4 - o) * 256, 256), 256)
        arrive("g2", o, grad_in.at[rows])

    def turned(pz, pc, message):
        both = dot(lt[pc * 4 + pz], grad_in[...])
        h_block[:, pl.ds(0, 512)] = both[0:128] + both[128:256]
        pack(lambda b: h_block[:, pl.ds(b * 128, 128)], message, 128, 4)

    for o in (2, 1, 3):
        for oc, pc in ((1, other), (0, core)):
            pz = turn(z, o)
            turned(pz, pc, h_out.at[o * 2 + oc])
            send("h1", o * 2 + oc, o * 2 + oc, h_out.at[o * 2 + oc], h_in.at[z, core], (x, y, pz, pc))
    turned(z, other, h_out.at[1])
    send("h1", 1, 1, h_out.at[1], h_in.at[z, core], (x, y, z, other))
    turned(z, core, h_in.at[z, core])

    def right_piece(py, pc):
        def one(px, carry):
            for b in range(2):
                v = decode(right_in[py, pc, px, pl.ds(b * 128, 128), :], BOUND)
                hi, lo = halves(v)
                rows = pl.ds(pl.multiple_of(py * 256 + (px // 2) * 128, 128), 128)
                at = pl.ds(pl.multiple_of((px % 2) * 512 + pc * 256 + b * 128, 128), 128)
                right_hi[rows, at] = hi
                right_lo[rows, at] = lo
            return carry

        lax.fori_loop(0, 4, one, 0)

    right_piece(y, core)
    for o in (1, 3, 2):
        py = turn(y, 4 - o)
        arrive("rg", o, right_in.at[py, core])
        send("rc", o, o, right_in.at[py, core], right_in.at[py, core], (x, y, z, other))
        right_piece(py, core)
    for o in (0, 1, 3, 2):
        py = turn(y, 4 - o)
        arrive("rc", o, right_in.at[py, other])
        right_piece(py, other)

    for o in range(4):
        for oc, pc in ((1, other), (0, core)):
            if o or oc:
                arrive("h1", o * 2 + oc, h_in.at[turn(z, 4 - o), pc])

    def h_sum(i, carry):
        pc, b = i // 4, i % 4
        v = None
        for pz in range(4):
            message = h_in.at[pz, pc]
            scale = message[pl.ds(512, 16), :].astype(F32)[0:1, :]
            term = decode(message[pl.ds(pl.multiple_of(b * 128, 128), 128), :], scale)
            v = term if v is None else v + term
        h_block[:, pl.ds(pl.multiple_of(i * 128, 128), 128)] = v
        return carry

    lax.fori_loop(0, 8, h_sum, 0)
    pack(lambda b: h_block[:, pl.ds(b * 128, 128)], h_gather_out, 128, 8)
    for o in (2, 1, 3):
        send("h2", o, o, h_gather_out, h_gather_in.at[z], (x, y, turn(z, o), core))

    order = (0, 1, 3, 2)

    def rotate(o):
        pz = turn(z, o)
        if o == 0:
            for b in range(8):
                hi, lo = halves(h_block[:, pl.ds(b * 128, 128)])
                h_parts[pl.ds(0, 128), pl.ds(b * 128, 128)] = hi
                h_parts[pl.ds(128, 128), pl.ds(b * 128, 128)] = lo
        else:
            arrive("h2", 4 - o, h_gather_in.at[pz])
            for b in range(8):
                hi, lo = halves(unpack(h_gather_in.at[pz], b, 128, 8))
                h_parts[pl.ds(0, 128), pl.ds(b * 128, 128)] = hi
                h_parts[pl.ds(128, 128), pl.ds(b * 128, 128)] = lo
        for i in (1, 2, 3, 0):
            jd = turn(xl * 2 + core, i)
            at = pl.ds(pl.multiple_of(jd * 256, 256), 256)
            both = dot(h_parts[...], right_hi[:, at])
            rot = both[0:128] + both[128:256] + dot(h_parts[pl.ds(0, 128), :], right_lo[:, at])
            pack(lambda b, rot=rot: rot[:, b * 128 : (b + 1) * 128], rot_out.at[o, i], 128, 2)
            target = (core * 2 + jd // 2, y, z, jd % 2)
            args = ("p", o * 4 + i, o * 4 + x, rot_out.at[o, i], rot_in.at[o, x], target)
            if i:
                send(*args)
            else:
                send_unless(xh == core, *args)

    def moments(o):
        for px in range(4):
            arrive("p", o * 4 + px, rot_in.at[o, px])
        rows = pl.ds(pl.multiple_of(turn(z, o) * 128, 128), 128)
        direction = []
        for b in range(2):
            rot = None
            for px in range(4):
                term = unpack(rot_in.at[o, px], b, 128, 2)
                rot = term if rot is None else rot + term
            at = pl.ds(b * 128, 128)
            moved_first = 0.9 * first[rows, at] + 0.1 * rot
            moved_second = 0.95 * second[rows, at] + 0.05 * rot * rot
            new_first[rows, at] = moved_first
            new_second[rows, at] = moved_second
            direction.append(
                moved_first / (1.0 - 0.9**STEP) / (jnp.sqrt(moved_second / (1.0 - 0.95**STEP)) + 1e-08)
            )
        pack(lambda b: direction[b], d_out.at[o], 128, 2)
        for i in (2, 1, 3, 0):
            args = ("d", o * 4 + i, o * 4 + xl * 2 + core, d_out.at[o], d_in.at[o, xl * 2 + core], (turn(x, i), y, z, xh))
            if i:
                send(*args)
            else:
                send_unless(xh == core, *args)

    def back(o):
        for j in range(4):
            arrive("d", o * 4 + j, d_in.at[o, j])
            for b in range(2):
                hi, lo = halves(unpack(d_in.at[o, j], b, 128, 2))
                at = pl.ds(j * 256 + b * 128, 128)
                d_parts[pl.ds(0, 128), at] = hi
                d_parts[pl.ds(128, 128), at] = lo

        def tile(i, carry):
            at = pl.ds(pl.multiple_of(i * 256, 256), 256)
            both = dot_t(d_parts[...], right_hi[at, :])
            v = both[0:128] + both[128:256] + dot_t(d_parts[pl.ds(0, 128), :], right_lo[at, :])
            y_block[:, at] = v
            return carry

        lax.fori_loop(0, 4, tile, 0)
        pz = turn(z, o)
        message = y_out.at[o] if o else y_in.at[z]
        pack(lambda b: y_block[:, pl.ds(b * 128, 128)], message, 128, 8)
        if o:
            send("y1", o, o, message, y_in.at[z], (x, y, pz, core))

    rotate(order[0])
    rotate(order[1])
    moments(order[0])
    rotate(order[2])
    moments(order[1])
    back(order[0])
    rotate(order[3])
    moments(order[2])
    back(order[1])
    moments(order[3])
    back(order[2])
    back(order[3])

    def flip(i, carry):
        chunk, s = i // 8, i % 8
        at = pl.ds(pl.multiple_of(s * 128, 128), 128)
        to = pl.ds(pl.multiple_of(chunk * 128, 128), 128)
        for part in range(2):
            v = lt[chunk, pl.ds(part * 128, 128), at].astype(F32).T.astype(BF16)
            lf[s // 2, pl.ds(pl.multiple_of(part * 256 + (s % 2) * 128, 128), 128), to] = v
        return carry

    lax.fori_loop(0, 64, flip, 0)

    for o in (1, 2, 3):
        arrive("y1", o, y_in.at[turn(z, 4 - o)])

    def y_sum(b, carry):
        v = None
        for pz in range(4):
            message = y_in.at[pz]
            scale = message[pl.ds(1024, 16), :].astype(F32)[0:1, :]
            term = decode(message[pl.ds(pl.multiple_of(b * 128, 128), 128), :], scale)
            v = term if v is None else v + term
        y_block[:, pl.ds(pl.multiple_of(b * 128, 128), 128)] = v
        return carry

    lax.fori_loop(0, 8, y_sum, 0)
    for half in range(2):
        pack(lambda b, half=half: y_block[:, pl.ds(half * 512 + b * 128, 128)], y_gather_out.at[half], 128, 4)
    for o in (2, 1, 3, 0):
        for oc, pc in ((1, other), (0, core)):
            if o or oc:
                send("y2", o * 2 + oc, o * 2 + oc, y_gather_out.at[pc], y_gather_in.at[core, z], (x, y, turn(z, o), pc))
    y_gather_in[core, z] = y_gather_out[core]

    def y_piece(pc, pz):
        rows = pl.ds(pl.multiple_of(pc * 512 + pz * 128, 128), 128)
        for b in range(4):
            hi, lo = halves(unpack(y_gather_in.at[pc, pz], b, 128, 4))
            y_hi[rows, pl.ds(b * 128, 128)] = hi
            y_lo[rows, pl.ds(b * 128, 128)] = lo

    y_piece(core, z)
    for o in (0, 1, 3, 2):
        for oc, pc in ((1, other), (0, core)):
            if o or oc:
                pz = turn(z, 4 - o)
                arrive("y2", o * 2 + oc, y_gather_in.at[pc, pz])
                y_piece(pc, pz)

    def raised(py, message):
        both = dot(lf[py], y_hi[...])
        u_block[...] = both[0:256] + both[256:512]
        u_block[...] += dot(lf[py, pl.ds(0, 256), :], y_lo[...])
        pack(lambda b: u_block[:, pl.ds(b * 128, 128)], message, 256, 4)

    for o in (2, 1, 3):
        py = turn(y, o)
        raised(py, u_out.at[o])
        send("u1", o, o, u_out.at[o], u_in.at[y], (x, py, z, core))
    raised(y, u_in.at[y])
    for o in (1, 2, 3):
        arrive("u1", o, u_in.at[turn(y, 4 - o)])

    def u_sum(b, carry):
        v = None
        for py in range(4):
            message = u_in.at[py]
            scale = message[pl.ds(1024, 16), :].astype(F32)[0:1, :]
            term = decode(message[pl.ds(pl.multiple_of(b * 256, 256), 256), :], scale)
            v = term if v is None else v + term
        u_block[:, pl.ds(pl.multiple_of(b * 128, 128), 128)] = v
        return carry

    lax.fori_loop(0, 4, u_sum, 0)
    for px in range(4):
        for pc in range(2):
            rows = pl.ds(px * 64 + pc * 32, 32)
            pack(lambda b, rows=rows: u_block[rows, pl.ds(b * 128, 128)], u_last_out.at[px, pc], 32, 4)
    for o in (2, 1, 3, 0):
        for oc, pc in ((1, other), (0, core)):
            if o or oc:
                px = turn(x, o)
                send("u2", o * 2 + oc, o * 2 + oc, u_last_out.at[px, pc], u_last_in.at[x, core], (px, y, z, pc))
    u_last_in[x, core] = u_last_out[x, core]
    for o in range(4):
        for oc, pc in ((1, other), (0, core)):
            if o or oc:
                arrive("u2", o * 2 + oc, u_last_in.at[turn(x, 4 - o), pc])
    for px in range(4):
        for pc in range(2):
            for b in range(4):
                update[:, pl.ds(pc * 2048 + b * 512 + px * 128, 128)] = unpack(u_last_in.at[px, pc], b, 32, 4)

    for wait in pending:
        wait()


def body(grad, left_basis, right_basis, first_moment, second_moment):
    vm = pltpu.VMEM
    scratch = [
        vm((4, 256, 128), BF16),
        vm((4, 2, 4, 256, 128), BF16),
        vm((8, 256, 1024), BF16),
        vm((4, 512, 1024), BF16),
        vm((4, 2, 32, 512), BF16),
        vm((1024, 512), BF16),
        vm((4, 256, 128), BF16),
        vm((4, 2, 4, 256, 128), BF16),
        vm((1024, 1024), BF16),
        vm((1024, 1024), BF16),
        vm((8, 528, 128), BF16),
        vm((4, 2, 528, 128), BF16),
        vm((1040, 128), BF16),
        vm((4, 1040, 128), BF16),
        vm((128, 1024), F32),
        vm((256, 1024), BF16),
        vm((4, 4, 272, 128), BF16),
        vm((4, 4, 272, 128), BF16),
        vm((4, 272, 128), BF16),
        vm((4, 4, 272, 128), BF16),
        vm((256, 1024), BF16),
        vm((128, 1024), F32),
        vm((4, 1040, 128), BF16),
        vm((4, 1040, 128), BF16),
        vm((2, 528, 128), BF16),
        vm((2, 4, 528, 128), BF16),
        vm((1024, 512), BF16),
        vm((1024, 512), BF16),
        vm((256, 512), F32),
        vm((4, 1040, 128), BF16),
        vm((4, 1040, 128), BF16),
        vm((4, 2, 144, 128), BF16),
        vm((4, 2, 144, 128), BF16),
        pltpu.SemaphoreType.DMA((104,)),
        pltpu.SemaphoreType.DMA((104,)),
    ]
    whole = pl.BlockSpec(memory_space=pltpu.VMEM)
    return pl.pallas_call(
        kernel,
        out_shape=(
            jax.ShapeDtypeStruct((32, 4096), F32),
            jax.ShapeDtypeStruct((512, 256), F32),
            jax.ShapeDtypeStruct((512, 256), F32),
        ),
        in_specs=[whole] * 5,
        out_specs=(whole,) * 3,
        scratch_shapes=scratch,
        compiler_params=pltpu.CompilerParams(
            collective_id=0, has_side_effects=True, vmem_limit_bytes=56 * 2**20
        ),
    )(grad, left_basis, right_basis, first_moment, second_moment)


def solution(mesh):
    placed = (
        P(("dp", "tensor"), None),
        P("dp", "tensor"),
        P("dp", "tensor"),
        P("dp", "tensor"),
        P("dp", "tensor"),
    )
    return jax.shard_map(
        body,
        mesh=mesh,
        in_specs=placed,
        out_specs=(P(("dp", "tensor"), None), P("dp", "tensor"), P("dp", "tensor")),
        check_vma=False,
    )
```

time: 704 us -> 158 us (0.22)
  the two profiles are of different devices: /device:TPU:1 before, /device:TPU:72 now
where the time goes in v1:
time: 158 us
  Pallas kernels  153 us (97%)
  local copies, waits for them, and re-layouts  3.95 us (2%)
    pallas_call x1, Pallas kernels, body(): pl.pallas_call(kernel, out_shape=(jax.ShapeDtypeStruct((32, 4096), F32),...  153 us
    unnamed x7, local copies, waits for them, and re-layouts  3.95 us

profile of v1, /device:TPU:72, one launch (start us, length us, event | category | flops | bytes accessed | tf_op | source)
XLA Modules:
  0.0 158.1 jit_solution(5787316004460401113)
XLA Ops:
  0.6 153.5 %shard_map.76 = (f32[32,4096]{1,0:T(8,128)}, f32[512,256]{1,0:T(8,128)}, f32[512,256]{1,0:T(8,128)}) custom-call(bf16[32,4096]{1,0:T(8,128)(2,1)} %grad.1, f32[512,256]{1,0:T(8,128)} %left.1, f32[512,256]{1,0:T(8,128)} %right.1, f32[512,256]{1,0:T(8,128)} %first.1, f32[512,256]{1,0:T(8,128)} %second.1), custom_call_target="tpu_custom_call" | custom-call | tf_op jit(solution)/shard_map/pallas_call | solution.py:502
  154.1 0.0 copy-start.1
  154.1 1.9 %copy.11 = f32[32,4096]{1,0:T(8,128)} copy(f32[32,4096]{1,0:T(8,128)} %get-tuple-element.6) | data formatting | bytes 1048576
  156.1 0.0 copy-done.1
  156.1 0.0 copy-start
  156.1 0.8 copy.12
  156.9 0.4 copy-done
  157.3 0.8 copy.13
Async XLA Ops:
  154.1 1.9 %copy-start.1 = (f32[512,256]{1,0:T(8,128)S(1)}, f32[512,256]{1,0:T(8,128)}, u32[]{:S(2)}) copy-start(f32[512,256]{1,0:T(8,128)} %get-tuple-element.7) | copy-start | bytes 1572868
  156.1 1.2 copy-start

commit v2 on v0

v2 whole, which is shorter than its diff:
```python
import jax
import jax.numpy as jnp
from jax import lax
from jax.experimental import pallas as pl
from jax.experimental.pallas import tpu as pltpu
from jax.sharding import PartitionSpec as P

STEP = 10
F32 = jnp.float32
BF16 = jnp.bfloat16
MESH = pl.DeviceIdType.MESH

SPAN = 250.0
BASE = 124.0
BOUND = 0.09375


def encode(x, inverse):
    t = jnp.maximum(jnp.abs(x) * inverse, 1e-30)
    y = jnp.exp2((t * lax.rsqrt(t)) * SPAN - BASE)
    return jnp.where(x < 0, -y, y).astype(BF16)


def decode(code, scale):
    y = code.astype(F32)
    t = (jnp.log2(jnp.abs(y)) + BASE) * (1.0 / SPAN)
    v = t * t * scale
    return jnp.where(y < 0, -v, v)


def pack(get, message, rows, blocks):
    most = None
    for b in range(blocks):
        a = jnp.abs(get(b))
        most = a if most is None else jnp.maximum(most, a)
    most = jnp.max(jnp.max(most, axis=0, keepdims=True), axis=1, keepdims=True)
    scale16 = (jnp.broadcast_to(most, (16, 128)) * 1.01 + 1e-30).astype(BF16)
    message[pl.ds(blocks * rows, 16), :] = scale16
    inverse = 1.0 / scale16.astype(F32)[0:1, :]
    for b in range(blocks):
        message[pl.ds(b * rows, rows), :] = encode(get(b), inverse)


def unpack(message, b, rows, blocks):
    scale = message[pl.ds(blocks * rows, 16), :].astype(F32)[0:1, :]
    return decode(message[pl.ds(b * rows, rows), :], scale)


def halves(x):
    hi = x.astype(BF16)
    return hi, (x - hi.astype(F32)).astype(BF16)


def dot(a, b):
    return lax.dot_general(a, b, (((1,), (0,)), ((), ())), preferred_element_type=F32)


def dot_t(a, b):
    return lax.dot_general(a, b, (((1,), (1,)), ((), ())), preferred_element_type=F32)


NC = 2
RC = 128 // NC


def kernel(
    grad, left, right, first, second, update, new_first, new_second,
    left_out, left_mid, left_in, lt, lf, grad_out, grad_in, right_out, right_in, right_hi, right_lo,
    h_out, h_in, h_gather, h_part, h_block, h_parts, rot_out, rot_in, d_block, d_out, d_in, d_parts,
    y_block, y_sum, y_out, y_in, y_gather_out, y_gather, y_hi, y_lo, u_acc, u_out, u_in, u_last_out, u_last_in,
    ss, rs,
):
    dp = lax.axis_index("dp")
    tensor = lax.axis_index("tensor")
    y, xh = dp // 2, dp % 2
    z, xl, core = tensor // 4, (tensor // 2) % 2, tensor % 2
    x = xh * 2 + xl
    other = 1 - core

    def device(px, py, pz, pc):
        return (py * 2 + px // 2, pz * 4 + (px % 2) * 2 + pc)

    def turn(a, o):
        return (a + o) % 4

    first_sem = {}
    total = 0
    for name, count in SEMAPHORES:
        first_sem[name] = total
        total += count

    pending = []

    def remote(name, i, j, src, dst, target):
        return pltpu.make_async_remote_copy(
            src_ref=src, dst_ref=dst, send_sem=ss.at[first_sem[name] + i], recv_sem=rs.at[first_sem[name] + j],
            device_id=device(*target), device_id_type=MESH,
        )

    def send(name, i, src, dst, target, j=None):
        copy = remote(name, i, i if j is None else j, src, dst, target)
        copy.start()
        pending.append(copy.wait_send)

    def send_unless(own, name, i, src, dst, target, j):
        here = pltpu.make_async_copy(src, dst, rs.at[first_sem[name] + j])
        there = remote(name, i, j, src, dst, target)
        pl.when(own)(here.start)
        pl.when(jnp.logical_not(own))(there.start)
        pending.append(lambda: pl.when(jnp.logical_not(own))(there.wait_send))

    def arrive(name, j, dst):
        pltpu.make_async_copy(dst, dst, rs.at[first_sem[name] + j]).wait()

    def both_cores(o):
        return [(oc, pc) for oc, pc in ((1, other), (0, core)) if o or oc]

    barrier = pltpu.get_barrier_semaphore()
    peers = [(turn(x, o), y, z, pc) for o in range(4) for _, pc in both_cores(o)]
    peers += [(x, y, turn(z, o), pc) for o in (1, 2, 3) for _, pc in both_cores(o)]
    peers += [(x, turn(y, o), z, core) for o in (1, 2, 3)]
    for peer in peers:
        pl.semaphore_signal(barrier, inc=1, device_id=device(*peer), device_id_type=MESH)

    for b in range(4):
        code = encode(left[pl.ds(b * 128, 128), :].T, 1.0 / BOUND)
        for a in range(NC):
            for h in range(2):
                left_out[a, b, pl.ds(h * RC, RC), :] = code[h * 128 + a * RC : h * 128 + (a + 1) * RC]
    for px in range(4):
        for pc in range(2):
            for b in range(4):
                grad_out[px, pc, :, pl.ds(b * 128, 128)] = grad[:, pl.ds(pc * 2048 + b * 512 + px * 128, 128)]

    pl.semaphore_wait(barrier, len(peers))

    for a in range(NC):
        for o in (2, 1, 3):
            send("lz", a * 4 + o, left_out.at[a, turn(z, o)], left_mid.at[a, z], (x, y, turn(z, o), core))
        left_mid[a, z] = left_out[a, z]
    own_rows = pl.ds(pl.multiple_of(y * 256 + x * 64 + core * 32, 32), 32)
    for o in (2, 1, 3, 0):
        for oc, pc in both_cores(o):
            px = turn(x, o)
            send("g1", o * 2 + oc, grad_out.at[px, pc], grad_in.at[own_rows], (px, y, z, pc))
    grad_in[own_rows] = grad_out[x, core]
    for q in range(4):
        for b in range(2):
            right_out[q, pl.ds(b * 128, 128), :] = encode(
                right[pl.ds(q * 128, 128), pl.ds(b * 128, 128)], 1.0 / BOUND
            )
    for o in (2, 1, 3):
        px = turn(x, o)
        send("r1", o, right_out.at[px], right_in.at[y, core, x], (px, y, z, core))
    right_in[y, core, x] = right_out[x]

    for a in range(NC):
        for o in (1, 2, 3):
            arrive("lz", a * 4 + o, left_mid.at[a, turn(z, 4 - o)])
        for o in (2, 1, 3):
            to = turn(y, o)
            send("ly", a * 4 + o, left_mid.at[a, to], left_in.at[a, x, core, y], (x, to, z, core))
        left_in[a, x, core, y] = left_mid[a, y]

    def left_spread(a):
        for o in (1, 2, 3):
            arrive("ly", a * 4 + o, left_in.at[a, x, core, turn(y, 4 - o)])
        piece = left_in.at[a, x, core]
        for o in (2, 1, 3):
            send("lg", a * 4 + o, piece, piece, (turn(x, o), y, z, core))
        send("lc", a * 4, piece, piece, (x, y, z, other))

    def left_piece(a, px, pc):
        def one(ry, carry):
            hi, lo = halves(decode(left_in[a, px, pc, ry], BOUND))
            at = pl.ds(pl.multiple_of(ry * 256 + (px // 2) * 128, 128), 128)
            for h in range(2):
                rows = (pc * 2 + h) * RC
                lt[a, px % 2, pl.ds(pl.multiple_of(rows, RC), RC), at] = hi[h * RC : (h + 1) * RC]
                lt[a, px % 2, pl.ds(pl.multiple_of(4 * RC + rows, RC), RC), at] = lo[h * RC : (h + 1) * RC]
            return carry

        lax.fori_loop(0, 4, one, 0)

    def left_forward(a):
        for o in (1, 3, 2):
            piece = left_in.at[a, turn(x, 4 - o), core]
            arrive("lg", a * 4 + o, piece)
            send("lc", a * 4 + o, piece, piece, (x, y, z, other))

    def left_take(a):
        for o in (0, 1, 3, 2):
            left_piece(a, turn(x, 4 - o), core)
        for o in (0, 1, 3, 2):
            px = turn(x, 4 - o)
            arrive("lc", a * 4 + o, left_in.at[a, px, other])
            left_piece(a, px, other)

    left_spread(0)
    for o in range(4):
        for oc, pc in both_cores(o):
            rows = pl.ds(pl.multiple_of(y * 256 + turn(x, 4 - o) * 64 + pc * 32, 32), 32)
            arrive("g1", o * 2 + oc, grad_in.at[rows])
    own_rows = pl.ds(pl.multiple_of(y * 256, 256), 256)
    for o in (2, 1, 3):
        send("g2", o, grad_in.at[own_rows], grad_in.at[own_rows], (x, turn(y, o), z, core))
    left_forward(0)
    left_spread(1)
    left_take(0)
    for o in (1, 2, 3):
        rows = pl.ds(pl.multiple_of(turn(y, 4 - o) * 256, 256), 256)
        arrive("g2", o, grad_in.at[rows])
    for o in (1, 2, 3):
        arrive("r1", o, right_in.at[y, core, turn(x, 4 - o)])
    piece = right_in.at[y, core]
    for o in (2, 1, 3):
        send("rg", o, piece, piece, (x, turn(y, o), z, core))
    send("rc", 0, piece, piece, (x, y, z, other))

    def turned(a):
        for oc, pc in ((1, other), (0, core)):
            both = dot(lt[a, pc], grad_in[...])
            h_block[...] = both[0 : 4 * RC] + both[4 * RC : 8 * RC]
            for o in (2, 1, 3, 0):
                pz = turn(z, o)
                rows = pl.ds(pl.multiple_of(pz * RC, RC), RC)
                message = h_out.at[a, o, oc] if o or oc else h_in.at[a, z, core]
                pack(lambda b, rows=rows: h_block[rows, pl.ds(b * 128, 128)], message, RC, 4)
                if o or oc:
                    send("h1", (a * 4 + o) * 2 + oc, message, h_in.at[a, z, core], (x, y, pz, pc))

    def turned_sum(a):
        for o in range(4):
            for oc, pc in both_cores(o):
                arrive("h1", (a * 4 + o) * 2 + oc, h_in.at[a, turn(z, 4 - o), pc])

        def one(b, carry):
            for pc in range(2):
                v = None
                for pz in range(4):
                    message = h_in.at[a, pz, pc]
                    scale = message[pl.ds(4 * RC, 16), :].astype(F32)[0:1, :]
                    term = decode(message[pl.ds(pl.multiple_of(b * RC, RC), RC), :], scale)
                    v = term if v is None else v + term
                h_part[:, pl.ds(pl.multiple_of(pc * 512 + b * 128, 128), 128)] = v
            return carry

        lax.fori_loop(0, 4, one, 0)
        message = h_gather.at[a, z]
        pack(lambda b: h_part[:, pl.ds(b * 128, 128)], message, RC, 8)
        for o in (2, 1, 3):
            send("h2", a * 4 + o, message, message, (x, y, turn(z, o), core))

    def rotate(a):
        for o in (1, 2, 3):
            arrive("h2", a * 4 + o, h_gather.at[a, turn(z, 4 - o)])

        def one(pz, carry):
            for b in range(8):
                hi, lo = halves(unpack(h_gather.at[a, pz], b, RC, 8))
                h_parts[pl.ds(pl.multiple_of(pz * RC, RC), RC), pl.ds(b * 128, 128)] = hi
                h_parts[pl.ds(pl.multiple_of((4 + pz) * RC, RC), RC), pl.ds(b * 128, 128)] = lo
            return carry

        lax.fori_loop(0, 4, one, 0)
        for i in (1, 2, 3, 0):
            jd = turn(xl * 2 + core, i)
            at = pl.ds(pl.multiple_of(jd * 256, 256), 256)
            both = dot(h_parts[...], right_hi[:, at])
            rot = both[0 : 4 * RC] + both[4 * RC : 8 * RC] + dot(h_parts[pl.ds(0, 4 * RC), :], right_lo[:, at])
            pack(lambda b, rot=rot: rot[:, b * 128 : (b + 1) * 128], rot_out.at[a, i], 4 * RC, 2)
            target = (core * 2 + jd // 2, y, z, jd % 2)
            args = ("p", a * 4 + i, rot_out.at[a, i], rot_in.at[a, x], target, a * 4 + x)
            if i:
                send(*args)
            else:
                send_unless(xh == core, *args)

    def moments(a):
        for px in range(4):
            arrive("p", a * 4 + px, rot_in.at[a, px])

        def one(pz, carry):
            rows = pl.ds(pl.multiple_of(pz * 128 + a * RC, RC), RC)
            part = pl.ds(pl.multiple_of(pz * RC, RC), RC)
            for b in range(2):
                rot = None
                for px in range(4):
                    message = rot_in.at[a, px]
                    scale = message[pl.ds(8 * RC, 16), :].astype(F32)[0:1, :]
                    term = decode(message[pl.ds(pl.multiple_of((b * 4 + pz) * RC, RC), RC), :], scale)
                    rot = term if rot is None else rot + term
                at = pl.ds(b * 128, 128)
                moved_first = 0.9 * first[rows, at] + 0.1 * rot
                moved_second = 0.95 * second[rows, at] + 0.05 * rot * rot
                new_first[rows, at] = moved_first
                new_second[rows, at] = moved_second
                d_block[part, at] = (
                    moved_first / (1.0 - 0.9**STEP) / (jnp.sqrt(moved_second / (1.0 - 0.95**STEP)) + 1e-08)
                )
            return carry

        lax.fori_loop(0, 4, one, 0)
        pack(lambda b: d_block[:, pl.ds(b * 128, 128)], d_out.at[a], 4 * RC, 2)
        slot = xl * 2 + core
        for i in (2, 1, 3, 0):
            args = ("d", a * 4 + i, d_out.at[a], d_in.at[a, slot], (turn(x, i), y, z, xh), a * 4 + slot)
            if i:
                send(*args)
            else:
                send_unless(xh == core, *args)

    def back(a):
        for j in range(4):
            arrive("d", a * 4 + j, d_in.at[a, j])
            for b in range(2):
                hi, lo = halves(unpack(d_in.at[a, j], b, 4 * RC, 2))
                at = pl.ds(j * 256 + b * 128, 128)
                d_parts[pl.ds(0, 4 * RC), at] = hi
                d_parts[pl.ds(4 * RC, 4 * RC), at] = lo

        def tile(i, carry):
            at = pl.ds(pl.multiple_of(i * 256, 256), 256)
            both = dot_t(d_parts[...], right_hi[at, :])
            low = dot_t(d_parts[pl.ds(0, 4 * RC), :], right_lo[at, :])
            y_block[:, at] = both[0 : 4 * RC] + both[4 * RC : 8 * RC] + low
            return carry

        lax.fori_loop(0, 4, tile, 0)
        for o in (2, 1, 3, 0):
            pz = turn(z, o)
            rows = pl.ds(pl.multiple_of(pz * RC, RC), RC)
            message = y_out.at[a, o] if o else y_in.at[a, z]
            pack(lambda b, rows=rows: y_block[rows, pl.ds(b * 128, 128)], message, RC, 8)
            if o:
                send("y1", a * 4 + o, message, y_in.at[a, z], (x, y, pz, core))

    def back_sum(a):
        for o in (1, 2, 3):
            arrive("y1", a * 4 + o, y_in.at[a, turn(z, 4 - o)])

        def one(b, carry):
            v = None
            for pz in range(4):
                message = y_in.at[a, pz]
                scale = message[pl.ds(8 * RC, 16), :].astype(F32)[0:1, :]
                term = decode(message[pl.ds(pl.multiple_of(b * RC, RC), RC), :], scale)
                v = term if v is None else v + term
            y_sum[:, pl.ds(pl.multiple_of(b * 128, 128), 128)] = v
            return carry

        lax.fori_loop(0, 8, one, 0)
        for oc, pc in ((1, other), (0, core)):
            message = y_gather_out.at[a] if oc else y_gather.at[a, core, z]
            pack(
                lambda b, pc=pc: y_sum[:, pl.ds(pl.multiple_of(pc * 512 + b * 128, 128), 128)], message, RC, 4
            )
            for o in (2, 1, 3, 0):
                if o or oc:
                    send("y2", (a * 4 + o) * 2 + oc, message, y_gather.at[a, core, z], (x, y, turn(z, o), pc))

    def flip(a):
        def one(i, carry):
            pc, s = i // 8, i % 8
            at = pl.ds(pl.multiple_of(s * 128, 128), 128)
            for part in range(2):
                for sub in range(4 * RC // 128):
                    rows = pl.ds(part * 4 * RC + sub * 128, 128)
                    v = lt[a, pc, rows, at].astype(F32).T.astype(BF16)
                    to = pl.ds(pl.multiple_of(part * 256 + (s % 2) * 128, 128), 128)
                    lf[a, s // 2, to, pl.ds(pl.multiple_of(pc * 4 * RC + sub * 128, 128), 128)] = v
            return carry

        lax.fori_loop(0, 16, one, 0)

    def raised_take(a):
        for o in range(4):
            for oc, pc in both_cores(o):
                arrive("y2", (a * 4 + o) * 2 + oc, y_gather.at[a, pc, turn(z, 4 - o)])

        def one(i, carry):
            rows = pl.ds(pl.multiple_of(i * RC, RC), RC)
            for b in range(4):
                hi, lo = halves(unpack(y_gather.at[a, i // 4, i % 4], b, RC, 4))
                y_hi[rows, pl.ds(b * 128, 128)] = hi
                y_lo[rows, pl.ds(b * 128, 128)] = lo
            return carry

        lax.fori_loop(0, 8, one, 0)

    def raised(a, py):
        both = dot(lf[a, py], y_hi[...])
        v = both[0:256] + both[256:512] + dot(lf[a, py, pl.ds(0, 256), :], y_lo[...])
        u_acc[py] = u_acc[py] + v if a else v

    turned(0)
    for a in range(1, NC):
        left_forward(a)
        if a + 1 < NC:
            left_spread(a + 1)
        left_take(a)
        turned(a)
    flip(0)
    turned_sum(0)

    def right_piece(py, pc):
        def one(px, carry):
            for b in range(2):
                hi, lo = halves(decode(right_in[py, pc, px, pl.ds(b * 128, 128), :], BOUND))
                rows = pl.ds(pl.multiple_of(py * 256 + (px // 2) * 128, 128), 128)
                at = pl.ds(pl.multiple_of((px % 2) * 512 + pc * 256 + b * 128, 128), 128)
                right_hi[rows, at] = hi
                right_lo[rows, at] = lo
            return carry

        lax.fori_loop(0, 4, one, 0)

    for o in (1, 3, 2):
        piece = right_in.at[turn(y, 4 - o), core]
        arrive("rg", o, piece)
        send("rc", o, piece, piece, (x, y, z, other))
    for o in (0, 1, 3, 2):
        right_piece(turn(y, 4 - o), core)
    for o in (0, 1, 3, 2):
        py = turn(y, 4 - o)
        arrive("rc", o, right_in.at[py, other])
        right_piece(py, other)

    for a in range(1, NC):
        turned_sum(a)
    for a in range(NC):
        rotate(a)
        if a + 1 < NC:
            flip(a + 1)
    for a in range(NC):
        moments(a)
    for a in range(NC):
        back(a)
    for a in range(NC):
        back_sum(a)
    for a in range(NC - 1):
        raised_take(a)

        def one(py, carry, a=a):
            raised(a, py)
            return carry

        lax.fori_loop(0, 4, one, 0)

    raised_take(NC - 1)
    for o in (2, 1, 3, 0):
        py = turn(y, o)
        raised(NC - 1, py)
        message = u_out.at[o] if o else u_in.at[y]
        pack(lambda b, py=py: u_acc[py, :, pl.ds(b * 128, 128)], message, 256, 4)
        if o:
            send("u1", o, message, u_in.at[y], (x, py, z, core))
    for o in (1, 2, 3):
        arrive("u1", o, u_in.at[turn(y, 4 - o)])

    def raised_sum(b, carry):
        v = None
        for py in range(4):
            message = u_in.at[py]
            scale = message[pl.ds(1024, 16), :].astype(F32)[0:1, :]
            term = decode(message[pl.ds(pl.multiple_of(b * 256, 256), 256), :], scale)
            v = term if v is None else v + term
        u_acc[0, :, pl.ds(pl.multiple_of(b * 128, 128), 128)] = v
        return carry

    lax.fori_loop(0, 4, raised_sum, 0)
    for px in range(4):
        for pc in range(2):
            rows = pl.ds(px * 64 + pc * 32, 32)
            pack(lambda b, rows=rows: u_acc[0, rows, pl.ds(b * 128, 128)], u_last_out.at[px, pc], 32, 4)
    for o in (2, 1, 3, 0):
        for oc, pc in both_cores(o):
            px = turn(x, o)
            send("u2", o * 2 + oc, u_last_out.at[px, pc], u_last_in.at[x, core], (px, y, z, pc))
    u_last_in[x, core] = u_last_out[x, core]
    for o in range(4):
        for oc, pc in both_cores(o):
            arrive("u2", o * 2 + oc, u_last_in.at[turn(x, 4 - o), pc])
    for px in range(4):
        for pc in range(2):
            for b in range(4):
                update[:, pl.ds(pc * 2048 + b * 512 + px * 128, 128)] = unpack(u_last_in.at[px, pc], b, 32, 4)

    for wait in pending:
        wait()


SEMAPHORES = (
    ("lz", 4 * NC), ("ly", 4 * NC), ("lg", 4 * NC), ("lc", 4 * NC), ("g1", 8), ("g2", 4),
    ("r1", 4), ("rg", 4), ("rc", 4), ("h1", 8 * NC), ("h2", 4 * NC), ("p", 4 * NC), ("d", 4 * NC),
    ("y1", 4 * NC), ("y2", 8 * NC), ("u1", 4), ("u2", 8),
)


def body(grad, left_basis, right_basis, first_moment, second_moment):
    vm = pltpu.VMEM
    count = sum(n for _, n in SEMAPHORES)
    scratch = [
        vm((NC, 4, 2 * RC, 128), BF16),
        vm((NC, 4, 2 * RC, 128), BF16),
        vm((NC, 4, 2, 4, 2 * RC, 128), BF16),
        vm((NC, 2, 8 * RC, 1024), BF16),
        vm((NC, 4, 512, 8 * RC), BF16),
        vm((4, 2, 32, 512), BF16),
        vm((1024, 512), BF16),
        vm((4, 256, 128), BF16),
        vm((4, 2, 4, 256, 128), BF16),
        vm((1024, 1024), BF16),
        vm((1024, 1024), BF16),
        vm((NC, 4, 2, 4 * RC + 16, 128), BF16),
        vm((NC, 4, 2, 4 * RC + 16, 128), BF16),
        vm((NC, 4, 8 * RC + 16, 128), BF16),
        vm((RC, 1024), F32),
        vm((4 * RC, 512), F32),
        vm((8 * RC, 1024), BF16),
        vm((NC, 4, 8 * RC + 16, 128), BF16),
        vm((NC, 4, 8 * RC + 16, 128), BF16),
        vm((4 * RC, 256), F32),
        vm((NC, 8 * RC + 16, 128), BF16),
        vm((NC, 4, 8 * RC + 16, 128), BF16),
        vm((8 * RC, 1024), BF16),
        vm((4 * RC, 1024), F32),
        vm((RC, 1024), F32),
        vm((NC, 4, 8 * RC + 16, 128), BF16),
        vm((NC, 4, 8 * RC + 16, 128), BF16),
        vm((NC, 4 * RC + 16, 128), BF16),
        vm((NC, 2, 4, 4 * RC + 16, 128), BF16),
        vm((8 * RC, 512), BF16),
        vm((8 * RC, 512), BF16),
        vm((4, 256, 512), F32),
        vm((4, 1040, 128), BF16),
        vm((4, 1040, 128), BF16),
        vm((4, 2, 144, 128), BF16),
        vm((4, 2, 144, 128), BF16),
        pltpu.SemaphoreType.DMA((count,)),
        pltpu.SemaphoreType.DMA((count,)),
    ]
    whole = pl.BlockSpec(memory_space=pltpu.VMEM)
    return pl.pallas_call(
        kernel,
        out_shape=(
            jax.ShapeDtypeStruct((32, 4096), F32),
            jax.ShapeDtypeStruct((512, 256), F32),
            jax.ShapeDtypeStruct((512, 256), F32),
        ),
        in_specs=[whole] * 5,
        out_specs=(whole,) * 3,
        scratch_shapes=scratch,
        compiler_params=pltpu.CompilerParams(
            collective_id=0, has_side_effects=True, vmem_limit_bytes=56 * 2**20
        ),
    )(grad, left_basis, right_basis, first_moment, second_moment)


def solution(mesh):
    placed = (
        P(("dp", "tensor"), None),
        P("dp", "tensor"),
        P("dp", "tensor"),
        P("dp", "tensor"),
        P("dp", "tensor"),
    )
    return jax.shard_map(
        body,
        mesh=mesh,
        in_specs=placed,
        out_specs=(P(("dp", "tensor"), None), P("dp", "tensor"), P("dp", "tensor")),
        check_vma=False,
    )
```

time: 704 us -> 135 us (0.19)
  waiting for transfers between devices: 600 us -> 0 us
  Pallas kernels: 0 us -> 129 us
  matrix products: 53.5 us -> 0 us
  blocking collectives: 29.7 us -> 0 us
  between operations: 14.2 us -> 0.65 us
    reduce_scatter x4 -> x0, waiting for transfers between devices: 356 us -> none  [the longest x1 94.6 us: body(): lax.psum_scatter(partial_update, 'tensor', scatter_dimension=1, tiled=True)]
    all_gather x4 -> x0, waiting for transfers between devices: 244 us -> none  [the longest x1 73.4 us: body(): gathered = lax.all_gather(half_back, 'dp', axis=0, tiled=True)]
    pallas_call x0 -> x1, Pallas kernels: none -> 129 us  [body(): pl.pallas_call(kernel, out_shape=(jax.ShapeDtypeStruct((32, 4096), F32),...]
    dot_general x4 -> x0, matrix products: 53.5 us -> none  [the longest x1 17 us: body(): jnp.einsum('ri,ci->rc', left_basis, gathered, precision=highest, preferre...]
    all_to_all x2 -> x0, blocking collectives: 29.7 us -> none  [the longest x1 14.9 us: body(): lax.all_to_all(summed, 'tensor', split_axis=0, concat_axis=1, tiled=True)]
  transfers between devices with their start and end apart: 8 -> 0, of which waited for: 8 -> 0; matrix products, arithmetic and copies ran while one was open for 0% -> 0% of each run, Pallas kernels for 0% -> 0%
where the time goes in v2:
time: 135 us; the launch traced here: 134 us
  Pallas kernels  129 us (96%)
  local copies, waits for them, and re-layouts  3.95 us (3%)
    pallas_call x1, Pallas kernels, body(): pl.pallas_call(kernel, out_shape=(jax.ShapeDtypeStruct((32, 4096), F32),...  129 us
    unnamed x7, local copies, waits for them, and re-layouts  3.95 us

profile of v2, /device:TPU:1, one launch (start us, length us, event | category | flops | bytes accessed | tf_op | source)
XLA Modules:
  0.0 133.7 jit_solution(17508621075917288879)
XLA Ops:
  0.6 129.1 %shard_map.76 = (f32[32,4096]{1,0:T(8,128)}, f32[512,256]{1,0:T(8,128)}, f32[512,256]{1,0:T(8,128)}) custom-call(bf16[32,4096]{1,0:T(8,128)(2,1)} %grad.1, f32[512,256]{1,0:T(8,128)} %left.1, f32[512,256]{1,0:T(8,128)} %right.1, f32[512,256]{1,0:T(8,128)} %first.1, f32[512,256]{1,0:T(8,128)} %second.1), custom_call_target="tpu_custom_call" | custom-call | tf_op jit(solution)/shard_map/pallas_call | solution.py:544
  129.7 0.0 copy-start.1
  129.7 1.9 %copy.11 = f32[32,4096]{1,0:T(8,128)} copy(f32[32,4096]{1,0:T(8,128)} %get-tuple-element.6) | data formatting | bytes 1048576
  131.6 0.0 copy-done.1
  131.7 0.0 copy-start
  131.7 0.8 copy.12
  132.4 0.4 copy-done
  132.9 0.8 copy.13
Async XLA Ops:
  129.7 1.9 %copy-start.1 = (f32[512,256]{1,0:T(8,128)S(1)}, f32[512,256]{1,0:T(8,128)}, u32[]{:S(2)}) copy-start(f32[512,256]{1,0:T(8,128)} %get-tuple-element.7) | copy-start | bytes 1572868
  131.7 1.2 copy-start

commit v3 on v2

--- a/solution.py
+++ b/solution.py
@@ -59,16 +59,20 @@
     return lax.dot_general(a, b, (((1,), (1,)), ((), ())), preferred_element_type=F32)
 
 
-NC = 2
+NC = 4
 RC = 128 // NC
+OFF = 1
+TIE = -1
+CC = 2
+CB = 4 // CC
 
 
 def kernel(
-    grad, left, right, first, second, update, new_first, new_second,
+    grad, left, right, first_hbm, second_hbm, u_last_in, first_out, second_out,
     left_out, left_mid, left_in, lt, lf, grad_out, grad_in, right_out, right_in, right_hi, right_lo,
-    h_out, h_in, h_gather, h_part, h_block, h_parts, rot_out, rot_in, d_block, d_out, d_in, d_parts,
-    y_block, y_sum, y_out, y_in, y_gather_out, y_gather, y_hi, y_lo, u_acc, u_out, u_in, u_last_out, u_last_in,
-    ss, rs,
+    h_out, h_in, h_gather, h_part, h_block, h_parts, rot_block, rot_out, rot_in, d_block, d_out, d_in, d_parts,
+    y_block, y_sum, y_out, y_in, y_gather_out, y_gather, y_hi, y_lo, u_acc, u_sum, u_out, u_in, u_last_out,
+    first, second, new_first, new_second, ss, rs, ls,
 ):
     dp = lax.axis_index("dp")
     tensor = lax.axis_index("tensor")
@@ -114,6 +118,10 @@
 
     def both_cores(o):
         return [(oc, pc) for oc, pc in ((1, other), (0, core)) if o or oc]
+
+    loads = [pltpu.make_async_copy(first_hbm, first, ls.at[0]), pltpu.make_async_copy(second_hbm, second, ls.at[1])]
+    for load in loads:
+        load.start()
 
     barrier = pltpu.get_barrier_semaphore()
     peers = [(turn(x, o), y, z, pc) for o in range(4) for _, pc in both_cores(o)]
@@ -154,7 +162,7 @@
         send("r1", o, right_out.at[px], right_in.at[y, core, x], (px, y, z, core))
     right_in[y, core, x] = right_out[x]
 
-    for a in range(NC):
+    def left_turn(a):
         for o in (1, 2, 3):
             arrive("lz", a * 4 + o, left_mid.at[a, turn(z, 4 - o)])
         for o in (2, 1, 3):
@@ -196,7 +204,8 @@
             arrive("lc", a * 4 + o, left_in.at[a, px, other])
             left_piece(a, px, other)
 
-    left_spread(0)
+    for a in range(NC):
+        left_turn(a)
     for o in range(4):
         for oc, pc in both_cores(o):
             rows = pl.ds(pl.multiple_of(y * 256 + turn(x, 4 - o) * 64 + pc * 32, 32), 32)
@@ -204,18 +213,23 @@
     own_rows = pl.ds(pl.multiple_of(y * 256, 256), 256)
     for o in (2, 1, 3):
         send("g2", o, grad_in.at[own_rows], grad_in.at[own_rows], (x, turn(y, o), z, core))
+    left_spread(0)
+    left_spread(1)
     left_forward(0)
-    left_spread(1)
     left_take(0)
-    for o in (1, 2, 3):
-        rows = pl.ds(pl.multiple_of(turn(y, 4 - o) * 256, 256), 256)
-        arrive("g2", o, grad_in.at[rows])
-    for o in (1, 2, 3):
-        arrive("r1", o, right_in.at[y, core, turn(x, 4 - o)])
-    piece = right_in.at[y, core]
-    for o in (2, 1, 3):
-        send("rg", o, piece, piece, (x, turn(y, o), z, core))
-    send("rc", 0, piece, piece, (x, y, z, other))
+
+    def basis_send():
+        for o in (1, 2, 3):
+            rows = pl.ds(pl.multiple_of(turn(y, 4 - o) * 256, 256), 256)
+            arrive("g2", o, grad_in.at[rows])
+        for o in (1, 2, 3):
+            arrive("r1", o, right_in.at[y, core, turn(x, 4 - o)])
+        piece = right_in.at[y, core]
+        for o in (2, 1, 3):
+            send("rg", o, piece, piece, (x, turn(y, o), z, core))
+        send("rc", 0, piece, piece, (x, y, z, other))
+
+    basis_send()
 
     def turned(a):
         for oc, pc in ((1, other), (0, core)):
@@ -263,12 +277,17 @@
             return carry
 
         lax.fori_loop(0, 4, one, 0)
+        for i in range(2):
+            at = pl.ds(i * 512, 512)
+            both = dot(h_parts[...], right_hi[:, at])
+            low = dot(h_parts[pl.ds(0, 4 * RC), :], right_lo[:, at])
+            rot_block[:, at] = both[0 : 4 * RC] + both[4 * RC : 8 * RC] + low
         for i in (1, 2, 3, 0):
             jd = turn(xl * 2 + core, i)
-            at = pl.ds(pl.multiple_of(jd * 256, 256), 256)
-            both = dot(h_parts[...], right_hi[:, at])
-            rot = both[0 : 4 * RC] + both[4 * RC : 8 * RC] + dot(h_parts[pl.ds(0, 4 * RC), :], right_lo[:, at])
-            pack(lambda b, rot=rot: rot[:, b * 128 : (b + 1) * 128], rot_out.at[a, i], 4 * RC, 2)
+            pack(
+                lambda b, jd=jd: rot_block[:, pl.ds(pl.multiple_of(jd * 256 + b * 128, 128), 128)],
+                rot_out.at[a, i], 4 * RC, 2,
+            )
             target = (core * 2 + jd // 2, y, z, jd % 2)
             args = ("p", a * 4 + i, rot_out.at[a, i], rot_in.at[a, x], target, a * 4 + x)
             if i:
@@ -277,6 +296,9 @@
                 send_unless(xh == core, *args)
 
     def moments(a):
+        if a == 0:
+            for load in loads:
+                load.wait()
         for px in range(4):
             arrive("p", a * 4 + px, rot_in.at[a, px])
 
@@ -302,6 +324,11 @@
 
         lax.fori_loop(0, 4, one, 0)
         pack(lambda b: d_block[:, pl.ds(b * 128, 128)], d_out.at[a], 4 * RC, 2)
+        if a == NC - 1:
+            for i, (src, dst) in enumerate(((new_first, first_out), (new_second, second_out))):
+                store = pltpu.make_async_copy(src, dst, ls.at[2 + i])
+                store.start()
+                pending.append(store.wait)
         slot = xl * 2 + core
         for i in (2, 1, 3, 0):
             args = ("d", a * 4 + i, d_out.at[a], d_in.at[a, slot], (turn(x, i), y, z, xh), a * 4 + slot)
@@ -320,13 +347,13 @@
                 d_parts[pl.ds(4 * RC, 4 * RC), at] = lo
 
         def tile(i, carry):
-            at = pl.ds(pl.multiple_of(i * 256, 256), 256)
+            at = pl.ds(pl.multiple_of(i * 512, 512), 512)
             both = dot_t(d_parts[...], right_hi[at, :])
             low = dot_t(d_parts[pl.ds(0, 4 * RC), :], right_lo[at, :])
             y_block[:, at] = both[0 : 4 * RC] + both[4 * RC : 8 * RC] + low
             return carry
 
-        lax.fori_loop(0, 4, tile, 0)
+        lax.fori_loop(0, 2, tile, 0)
         for o in (2, 1, 3, 0):
             pz = turn(z, o)
             rows = pl.ds(pl.multiple_of(pz * RC, RC), RC)
@@ -393,16 +420,6 @@
         v = both[0:256] + both[256:512] + dot(lf[a, py, pl.ds(0, 256), :], y_lo[...])
         u_acc[py] = u_acc[py] + v if a else v
 
-    turned(0)
-    for a in range(1, NC):
-        left_forward(a)
-        if a + 1 < NC:
-            left_spread(a + 1)
-        left_take(a)
-        turned(a)
-    flip(0)
-    turned_sum(0)
-
     def right_piece(py, pc):
         def one(px, carry):
             for b in range(2):
@@ -415,85 +432,110 @@
 
         lax.fori_loop(0, 4, one, 0)
 
-    for o in (1, 3, 2):
-        piece = right_in.at[turn(y, 4 - o), core]
-        arrive("rg", o, piece)
-        send("rc", o, piece, piece, (x, y, z, other))
-    for o in (0, 1, 3, 2):
-        right_piece(turn(y, 4 - o), core)
-    for o in (0, 1, 3, 2):
-        py = turn(y, 4 - o)
-        arrive("rc", o, right_in.at[py, other])
-        right_piece(py, other)
-
-    for a in range(1, NC):
-        turned_sum(a)
-    for a in range(NC):
-        rotate(a)
-        if a + 1 < NC:
-            flip(a + 1)
-    for a in range(NC):
-        moments(a)
-    for a in range(NC):
-        back(a)
-    for a in range(NC):
-        back_sum(a)
-    for a in range(NC - 1):
-        raised_take(a)
-
-        def one(py, carry, a=a):
-            raised(a, py)
-            return carry
-
-        lax.fori_loop(0, 4, one, 0)
+    def basis_take():
+        for o in (1, 3, 2):
+            piece = right_in.at[turn(y, 4 - o), core]
+            arrive("rg", o, piece)
+            send("rc", o, piece, piece, (x, y, z, other))
+        for o in (0, 1, 3, 2):
+            right_piece(turn(y, 4 - o), core)
+        for o in (0, 1, 3, 2):
+            py = turn(y, 4 - o)
+            arrive("rc", o, right_in.at[py, other])
+            right_piece(py, other)
+
+    def step(stage, a):
+        if stage == 0:
+            if a:
+                left_forward(a)
+            if a + 2 < NC:
+                left_spread(a + 2)
+            if a:
+                left_take(a)
+            turned(a)
+        if stage == 1:
+            flip(a)
+            turned_sum(a)
+        if stage == 2:
+            if a == 0:
+                basis_take()
+            rotate(a)
+        if stage == 3:
+            moments(a)
+        if stage == 4:
+            back(a)
+        if stage == 5:
+            back_sum(a)
+        if stage == 6 and a < NC - 1:
+            raised_take(a)
+
+            def one(py, carry, a=a):
+                raised(a, py)
+                return carry
+
+            lax.fori_loop(0, 4, one, 0)
+
+    for _, _, stage, a in sorted((s + OFF * a, TIE * a, s, a) for s in range(7) for a in range(NC)):
+        step(stage, a)
 
     raised_take(NC - 1)
     for o in (2, 1, 3, 0):
         py = turn(y, o)
         raised(NC - 1, py)
-        message = u_out.at[o] if o else u_in.at[y]
-        pack(lambda b, py=py: u_acc[py, :, pl.ds(b * 128, 128)], message, 256, 4)
-        if o:
-            send("u1", o, message, u_in.at[y], (x, py, z, core))
-    for o in (1, 2, 3):
-        arrive("u1", o, u_in.at[turn(y, 4 - o)])
-
-    def raised_sum(b, carry):
-        v = None
-        for py in range(4):
-            message = u_in.at[py]
-            scale = message[pl.ds(1024, 16), :].astype(F32)[0:1, :]
-            term = decode(message[pl.ds(pl.multiple_of(b * 256, 256), 256), :], scale)
-            v = term if v is None else v + term
-        u_acc[0, :, pl.ds(pl.multiple_of(b * 128, 128), 128)] = v
-        return carry
-
-    lax.fori_loop(0, 4, raised_sum, 0)
-    for px in range(4):
-        for pc in range(2):
-            rows = pl.ds(px * 64 + pc * 32, 32)
-            pack(lambda b, rows=rows: u_acc[0, rows, pl.ds(b * 128, 128)], u_last_out.at[px, pc], 32, 4)
-    for o in (2, 1, 3, 0):
-        for oc, pc in both_cores(o):
-            px = turn(x, o)
-            send("u2", o * 2 + oc, u_last_out.at[px, pc], u_last_in.at[x, core], (px, y, z, pc))
-    u_last_in[x, core] = u_last_out[x, core]
-    for o in range(4):
-        for oc, pc in both_cores(o):
-            arrive("u2", o * 2 + oc, u_last_in.at[turn(x, 4 - o), pc])
-    for px in range(4):
-        for pc in range(2):
-            for b in range(4):
-                update[:, pl.ds(pc * 2048 + b * 512 + px * 128, 128)] = unpack(u_last_in.at[px, pc], b, 32, 4)
-
+        for c in range(CC):
+            message = u_out.at[c, o] if o else u_in.at[c, y]
+            pack(lambda b, py=py, c=c: u_acc[py, :, pl.ds((c * CB + b) * 128, 128)], message, 256, CB)
+            if o:
+                send("u1", c * 4 + o, message, u_in.at[c, y], (x, py, z, core))
+    for c in range(CC):
+        for o in (1, 2, 3):
+            arrive("u1", c * 4 + o, u_in.at[c, turn(y, 4 - o)])
+
+        def raised_sum(b, carry, c=c):
+            v = None
+            for py in range(4):
+                message = u_in.at[c, py]
+                scale = message[pl.ds(256 * CB, 16), :].astype(F32)[0:1, :]
+                term = decode(message[pl.ds(pl.multiple_of(b * 256, 256), 256), :], scale)
+                v = term if v is None else v + term
+            u_sum[:, pl.ds(pl.multiple_of(b * 128, 128), 128)] = v
+            return carry
+
+        lax.fori_loop(0, CB, raised_sum, 0)
+        for px in range(4):
+            for pc in range(2):
+                rows = pl.ds(px * 64 + pc * 32, 32)
+                pack(lambda b, rows=rows: u_sum[rows, pl.ds(b * 128, 128)], u_last_out.at[c, px, pc], 32, CB)
+        for o in (2, 1, 3, 0):
+            for oc, pc in both_cores(o):
+                px = turn(x, o)
+                send("u2", (c * 4 + o) * 2 + oc, u_last_out.at[c, px, pc], u_last_in.at[c, x, core], (px, y, z, pc))
+        own = pltpu.make_async_copy(u_last_out.at[c, x, core], u_last_in.at[c, x, core], ls.at[4 + c])
+        own.start()
+        pending.append(own.wait)
+    for c in range(CC):
+        for o in range(4):
+            for oc, pc in both_cores(o):
+                arrive("u2", (c * 4 + o) * 2 + oc, u_last_in.at[c, turn(x, 4 - o), pc])
     for wait in pending:
         wait()
+
+
+def finish(coded, first, second, update, new_first, new_second):
+    new_first[...] = first[...]
+    new_second[...] = second[...]
+    for c in range(CC):
+        for px in range(4):
+            for pc in range(2):
+                for b in range(CB):
+                    at = pl.ds(pc * 2048 + (c * CB + b) * 512 + px * 128, 128)
+                    update[:, at] = unpack(coded.at[c, px, pc], b, 32, CB)
 
 
 SEMAPHORES = (
     ("lz", 4 * NC), ("ly", 4 * NC), ("lg", 4 * NC), ("lc", 4 * NC), ("g1", 8), ("g2", 4),
     ("r1", 4), ("rg", 4), ("rc", 4), ("h1", 8 * NC), ("h2", 4 * NC), ("p", 4 * NC), ("d", 4 * NC),
-    ("y1", 4 * NC), ("y2", 8 * NC), ("u1", 4), ("u2", 8),
+    ("y1", 4 * NC), ("y2", 8 * NC), ("u1", 4 * CC), ("u2", 8 * CC),
 )
 
 
@@ -518,6 +560,7 @@
         vm((RC, 1024), F32),
         vm((4 * RC, 512), F32),
         vm((8 * RC, 1024), BF16),
+        vm((4 * RC, 1024), F32),
         vm((NC, 4, 8 * RC + 16, 128), BF16),
         vm((NC, 4, 8 * RC + 16, 128), BF16),
         vm((4 * RC, 256), F32),
@@ -533,28 +576,37 @@
         vm((8 * RC, 512), BF16),
         vm((8 * RC, 512), BF16),
         vm((4, 256, 512), F32),
-        vm((4, 1040, 128), BF16),
-        vm((4, 1040, 128), BF16),
-        vm((4, 2, 144, 128), BF16),
-        vm((4, 2, 144, 128), BF16),
+        vm((256, 128 * CB), F32),
+        vm((CC, 4, 256 * CB + 16, 128), BF16),
+        vm((CC, 4, 256 * CB + 16, 128), BF16),
+        vm((CC, 4, 2, 32 * CB + 16, 128), BF16),
+        vm((512, 256), F32),
+        vm((512, 256), F32),
+        vm((512, 256), F32),
+        vm((512, 256), F32),
         pltpu.SemaphoreType.DMA((count,)),
         pltpu.SemaphoreType.DMA((count,)),
+        pltpu.SemaphoreType.DMA((4 + CC,)),
     ]
     whole = pl.BlockSpec(memory_space=pltpu.VMEM)
-    return pl.pallas_call(
+    there = pl.BlockSpec(memory_space=pl.ANY)
+    square = jax.ShapeDtypeStruct((512, 256), F32)
+    coded, new_first, new_second = pl.pallas_call(
         kernel,
-        out_shape=(
-            jax.ShapeDtypeStruct((32, 4096), F32),
-            jax.ShapeDtypeStruct((512, 256), F32),
-            jax.ShapeDtypeStruct((512, 256), F32),
-        ),
-        in_specs=[whole] * 5,
-        out_specs=(whole,) * 3,
+        out_shape=(jax.ShapeDtypeStruct((CC, 4, 2, 32 * CB + 16, 128), BF16), square, square),
+        in_specs=[whole, whole, whole, there, there],
+        out_specs=(there,) * 3,
         scratch_shapes=scratch,
         compiler_params=pltpu.CompilerParams(
             collective_id=0, has_side_effects=True, vmem_limit_bytes=56 * 2**20
         ),
     )(grad, left_basis, right_basis, first_moment, second_moment)
+    return pl.pallas_call(
+        finish,
+        out_shape=(jax.ShapeDtypeStruct((32, 4096), F32), square, square),
+        in_specs=[whole] * 3,
+        out_specs=(whole,) * 3,
+    )(coded, new_first, new_second)
 
 
 def solution(mesh):

time: 135 us -> 121 us (0.90)
  Pallas kernels: 129 us -> 120 us
  local copies, waits for them, and re-layouts: 3.95 us -> 0 us
    pallas_call x1 -> x2, Pallas kernels: 129 us -> 120 us  [the longest x1 118 us: body(): pl.pallas_call(kernel, out_shape=(jax.ShapeDtypeStruct((CC, 4, 2, 32 * CB...]
    unnamed x7 -> x0, local copies, waits for them, and re-layouts: 3.95 us -> none
where the time goes in v3:
time: 121 us
  Pallas kernels  120 us (99%)
    pallas_call x1, Pallas kernels, body(): pl.pallas_call(kernel, out_shape=(jax.ShapeDtypeStruct((CC, 4, 2, 32 * CB...  118 us
    pallas_call x1, Pallas kernels, body(): pl.pallas_call(finish, out_shape=(jax.ShapeDtypeStruct((32, 4096), F32),...  2.47 us

profile of v3, /device:TPU:1, one launch (start us, length us, event | category | flops | bytes accessed | tf_op | source)
XLA Modules:
  0.0 120.7 jit_solution(12654156853570189281)
XLA Ops:
  0.6 117.6 %shard_map.76 = (bf16[2,4,2,80,128]{4,3,2,1,0:T(8,128)(2,1)}, f32[512,256]{1,0:T(8,128)}, f32[512,256]{1,0:T(8,128)}) custom-call(bf16[32,4096]{1,0:T(8,128)(2,1)} %grad.1, f32[512,256]{1,0:T(8,128)} %left.1, f32[512,256]{1,0:T(8,128)} %right.1, f32[512,256]{1,0:T(8,128)} %first_hbm.1, f32[512,256]{1,0:T(8,128)} %second_hbm.1), custom_call_target="tpu_custom_call" | custom-call | tf_op jit(solution)/shard_map/pallas_call | solution.py:594
  118.3 2.5 %shard_map.77 = (f32[32,4096]{1,0:T(8,128)}, f32[512,256]{1,0:T(8,128)}, f32[512,256]{1,0:T(8,128)}) custom-call(bf16[2,4,2,80,128]{4,3,2,1,0:T(8,128)(2,1)} %get-tuple-element.6.coded, f32[512,256]{1,0:T(8,128)} %get-tuple-element.7.first, f32[512,256]{1,0:T(8,128)} %get-tuple-element.8.second), custom_call_target="tpu_custom_call" | custom-call | tf_op jit(solution)/shard_map/pallas_call | solution.py:604

commit v4 on v3

v4 whole, which is shorter than its diff:
```python
import functools

import jax
import jax.numpy as jnp
from jax import lax
from jax.experimental import pallas as pl
from jax.experimental.pallas import tpu as pltpu
from jax.sharding import PartitionSpec as P

STEP = 10
F32 = jnp.float32
BF16 = jnp.bfloat16
MESH = pl.DeviceIdType.MESH

SPAN = 250.0
BASE = 124.0
BOUND = 0.09375


def encode(x, inverse):
    t = jnp.maximum(jnp.abs(x) * inverse, 1e-30)
    y = jnp.exp2((t * lax.rsqrt(t)) * SPAN - BASE)
    return jnp.where(x < 0, -y, y).astype(BF16)


def decode(code, scale):
    y = code.astype(F32)
    t = (jnp.log2(jnp.abs(y)) + BASE) * (1.0 / SPAN)
    v = t * t * scale
    return jnp.where(y < 0, -v, v)


def pack(get, message, rows, blocks):
    most = None
    for b in range(blocks):
        a = jnp.max(jnp.abs(get(b)).reshape(rows // 16, 16, 128), axis=0)
        most = a if most is None else jnp.maximum(most, a)
    scale = (most * 1.01 + 1e-30).astype(BF16)
    message[pl.ds(blocks * rows, 16), :] = scale
    inverse = (1.0 / scale.astype(F32))[None]
    for b in range(blocks):
        code = encode(get(b).reshape(rows // 16, 16, 128), inverse)
        message[pl.ds(b * rows, rows), :] = code.reshape(rows, 128)


def unpack_rows(message, start, rows, end):
    scale = message[pl.ds(end, 16), :].astype(F32)[None]
    code = message[pl.ds(start, rows), :].reshape(rows // 16, 16, 128)
    return decode(code, scale).reshape(rows, 128)


def unpack(message, b, rows, blocks):
    return unpack_rows(message, b * rows, rows, blocks * rows)


def halves(x):
    hi = x.astype(BF16)
    return hi, (x - hi.astype(F32)).astype(BF16)


def dot(a, b):
    return lax.dot_general(a, b, (((1,), (0,)), ((), ())), preferred_element_type=F32)


def dot_t(a, b):
    return lax.dot_general(a, b, (((1,), (1,)), ((), ())), preferred_element_type=F32)


NC = 4
RC = 128 // NC
OFF = 1
EARLY = 2
TIE = -1
CC = 4
CB = 4 // CC


def kernel(
    grad, left, right, first_hbm, second_hbm, u_last_in, first_out, second_out,
    left_out, left_mid, left_in, lt, lf, grad_out, grad_in, right_out, right_in, right_hi, right_lo,
    h_out, h_in, h_gather, h_part, h_block, h_parts, rot_block, rot_out, rot_in, d_block, d_out, d_in, d_parts,
    y_block, y_sum, y_out, y_in, y_gather_out, y_gather, y_hi, y_lo, u_acc, u_sum, u_out, u_in, u_last_out,
    first, second, new_first, new_second, ss, rs, ls,
):
    dp = lax.axis_index("dp")
    tensor = lax.axis_index("tensor")
    y, xh = dp // 2, dp % 2
    z, xl, core = tensor // 4, (tensor // 2) % 2, tensor % 2
    x = xh * 2 + xl
    other = 1 - core

    def device(px, py, pz, pc):
        return (py * 2 + px // 2, pz * 4 + (px % 2) * 2 + pc)

    def turn(a, o):
        return (a + o) % 4

    first_sem, send_sem = {}, {}
    total = 0
    for i, (name, count) in enumerate(SEMAPHORES):
        first_sem[name], send_sem[name] = total, i
        total += count

    def remote(name, j, src, dst, target):
        return pltpu.make_async_remote_copy(
            src_ref=src, dst_ref=dst, send_sem=ss.at[send_sem[name]], recv_sem=rs.at[first_sem[name] + j],
            device_id=device(*target), device_id_type=MESH,
        )

    def send(name, j, src, dst, target):
        remote(name, j, src, dst, target).start()

    def send_unless(own, name, j, src, dst, target):
        pl.when(own)(pltpu.make_async_copy(src, dst, rs.at[first_sem[name] + j]).start)
        pl.when(jnp.logical_not(own))(remote(name, j, src, dst, target).start)

    def arrive(name, j, like):
        pltpu.make_async_copy(like, like, rs.at[first_sem[name] + j]).wait()

    def sent(name, like):
        pltpu.make_async_copy(like, like, ss.at[send_sem[name]]).wait()

    def both_cores(o):
        return [(oc, pc) for oc, pc in ((1, other), (0, core)) if o or oc]

    pending = []
    loads = [pltpu.make_async_copy(first_hbm, first, ls.at[0]), pltpu.make_async_copy(second_hbm, second, ls.at[1])]
    for load in loads:
        load.start()

    barrier = pltpu.get_barrier_semaphore()
    peers = [(turn(x, o), y, z, pc) for o in range(4) for _, pc in both_cores(o)]
    peers += [(x, y, turn(z, o), pc) for o in (1, 2, 3) for _, pc in both_cores(o)]
    peers += [(x, turn(y, o), z, core) for o in (1, 2, 3)]
    for peer in peers:
        pl.semaphore_signal(barrier, inc=1, device_id=device(*peer), device_id_type=MESH)

    for b in range(4):
        code = encode(left[pl.ds(b * 128, 128), :].T, 1.0 / BOUND)
        for a in range(NC):
            for h in range(2):
                left_out[a, b, pl.ds(h * RC, RC), :] = code[h * 128 + a * RC : h * 128 + (a + 1) * RC]
    for px in range(4):
        for pc in range(2):
            for b in range(4):
                grad_out[px, pc, :, pl.ds(b * 128, 128)] = grad[:, pl.ds(pc * 2048 + b * 512 + px * 128, 128)]

    pl.semaphore_wait(barrier, len(peers))

    for a in range(NC):
        for o in (2, 1, 3):
            send("lz", a, left_out.at[a, turn(z, o)], left_mid.at[a, z], (x, y, turn(z, o), core))
        left_mid[a, z] = left_out[a, z]
    own_rows = pl.ds(pl.multiple_of(y * 256 + x * 64 + core * 32, 32), 32)
    for o in (2, 1, 3, 0):
        for oc, pc in both_cores(o):
            px = turn(x, o)
            send("g1", 0, grad_out.at[px, pc], grad_in.at[own_rows], (px, y, z, pc))
    grad_in[own_rows] = grad_out[x, core]
    for q in range(4):
        for b in range(2):
            right_out[q, pl.ds(b * 128, 128), :] = encode(
                right[pl.ds(q * 128, 128), pl.ds(b * 128, 128)], 1.0 / BOUND
            )
    for o in (2, 1, 3):
        px = turn(x, o)
        send("r1", 0, right_out.at[px], right_in.at[y, core, x], (px, y, z, core))
    right_in[y, core, x] = right_out[x]

    def ring_start(name, half):
        for up, h, part in ((1, 0, 0), (3, 1, 1), (1, 1, 2), (3, 0, 2)):
            send(name, part, half(y, h), half(y, h), (x, turn(y, up), z, core))

    def ring_pass(name, half):
        for from_, h, to in ((3, 0, 1), (1, 1, 3)):
            piece = half(turn(y, from_), h)
            arrive(name, h, piece)
            send(name, 2, piece, piece, (x, turn(y, to), z, core))

    def grad_half(py, h):
        return grad_in.at[pl.ds(pl.multiple_of(py * 256 + h * 128, 128), 128)]

    def right_half(py, h):
        return right_in.at[py, core, pl.ds(h * 2, 2)]

    def left_turn(a):
        arrive("lz", a, left_mid.at[a, pl.ds(0, 3)])
        for o in (2, 1, 3):
            to = turn(y, o)
            send("ly", a, left_mid.at[a, to], left_in.at[a, x, core, y], (x, to, z, core))
        left_in[a, x, core, y] = left_mid[a, y]

    def left_spread(a):
        piece = left_in.at[a, x, core]
        arrive("ly", a, piece.at[pl.ds(0, 3)])
        for o in (2, 1, 3):
            send("lg", a, piece, piece, (turn(x, o), y, z, core))
        send("lc", a, piece, piece, (x, y, z, other))

    def left_forward(a):
        arrive("lg", a, left_in.at[a, pl.ds(0, 3), core])
        for o in (1, 3, 2):
            piece = left_in.at[a, turn(x, 4 - o), core]
            send("lc", a, piece, piece, (x, y, z, other))

    def left_take(a):
        def one(px, carry, pc):
            for ry in range(4):
                hi, lo = halves(decode(left_in[a, px, pc, ry], BOUND))
                at = pl.ds(pl.multiple_of(ry * 256 + (px // 2) * 128, 128), 128)
                for h in range(2):
                    rows = (pc * 2 + h) * RC
                    lt[a, px % 2, pl.ds(pl.multiple_of(rows, RC), RC), at] = hi[h * RC : (h + 1) * RC]
                    lt[a, px % 2, pl.ds(pl.multiple_of(4 * RC + rows, RC), RC), at] = lo[h * RC : (h + 1) * RC]
            return carry

        lax.fori_loop(0, 4, functools.partial(one, pc=core), 0)
        arrive("lc", a, left_in.at[a, :, other])
        lax.fori_loop(0, 4, functools.partial(one, pc=other), 0)

    def flip(a):
        def one(s, carry):
            at = pl.ds(pl.multiple_of(s * 128, 128), 128)
            for pc in range(2):
                for part in range(2):
                    for sub in range(4 * RC // 128):
                        v = lt[a, pc, pl.ds(part * 4 * RC + sub * 128, 128), at].T
                        to = pl.ds(pl.multiple_of(part * 256 + (s % 2) * 128, 128), 128)
                        lf[a, s // 2, to, pl.ds(pc * 4 * RC + sub * 128, 128)] = v
            return carry

        lax.fori_loop(0, 8, one, 0)

    for a in range(NC):
        left_turn(a)
    arrive("g1", 0, grad_in.at[pl.ds(0, 224)])
    ring_start("g2", grad_half)
    left_spread(0)
    left_spread(1)
    ring_pass("g2", grad_half)
    arrive("r1", 0, right_in.at[0, 0, pl.ds(0, 3)])
    ring_start("rg", right_half)
    send("rc", 0, right_in.at[y, core], right_in.at[y, core], (x, y, z, other))
    left_forward(0)
    left_spread(2)
    left_take(0)
    flip(0)
    for a in range(1, EARLY):
        left_forward(a)
        if a + 2 < NC:
            left_spread(a + 2)
        left_take(a)
        flip(a)
    arrive("g2", 2, grad_in.at[pl.ds(0, 512)])

    def turned(a):
        for oc, pc in ((1, other), (0, core)):
            both = dot(lt[a, pc], grad_in[...])
            h_block[...] = both[0 : 4 * RC] + both[4 * RC : 8 * RC]
            for o in (2, 1, 3, 0):
                pz = turn(z, o)
                rows = pl.ds(pl.multiple_of(pz * RC, RC), RC)
                here = h_in.at[a, z * 2 + core]
                message = h_out.at[a, o, oc] if o or oc else here
                pack(lambda b, rows=rows: h_block[rows, pl.ds(b * 128, 128)], message, RC, 4)
                if o or oc:
                    send("h1", a, message, here, (x, y, pz, pc))

    def turned_sum(a):
        arrive("h1", a, h_in.at[a, pl.ds(0, 7)])

        def one(b, carry):
            for pc in range(2):
                v = None
                for pz in range(4):
                    start = pl.multiple_of(b * RC, RC)
                    term = unpack_rows(h_in.at[a, pz * 2 + pc], start, RC, 4 * RC)
                    v = term if v is None else v + term
                h_part[:, pl.ds(pl.multiple_of(pc * 512 + b * 128, 128), 128)] = v
            return carry

        lax.fori_loop(0, 4, one, 0)
        message = h_gather.at[a, z]
        pack(lambda b: h_part[:, pl.ds(b * 128, 128)], message, RC, 8)
        for o in (2, 1, 3):
            send("h2", a, message, message, (x, y, turn(z, o), core))

    def rotate(a):
        arrive("h2", a, h_gather.at[a, pl.ds(0, 3)])

        def one(pz, carry):
            for b in range(8):
                hi, lo = halves(unpack(h_gather.at[a, pz], b, RC, 8))
                h_parts[pl.ds(pl.multiple_of(pz * RC, RC), RC), pl.ds(b * 128, 128)] = hi
                h_parts[pl.ds(pl.multiple_of((4 + pz) * RC, RC), RC), pl.ds(b * 128, 128)] = lo
            return carry

        lax.fori_loop(0, 4, one, 0)
        for i in range(2):
            at = pl.ds(i * 512, 512)
            both = dot(h_parts[...], right_hi[:, at])
            low = dot(h_parts[pl.ds(0, 4 * RC), :], right_lo[:, at])
            rot_block[:, at] = both[0 : 4 * RC] + both[4 * RC : 8 * RC] + low
        for i in (1, 2, 3, 0):
            jd = turn(xl * 2 + core, i)
            pack(
                lambda b, jd=jd: rot_block[:, pl.ds(pl.multiple_of(jd * 256 + b * 128, 128), 128)],
                rot_out.at[a, i], 4 * RC, 2,
            )
            target = (core * 2 + jd // 2, y, z, jd % 2)
            args = ("p", a, rot_out.at[a, i], rot_in.at[a, x], target)
            if i:
                send(*args)
            else:
                send_unless(xh == core, *args)

    def moments(a):
        if a == 0:
            for load in loads:
                load.wait()
        arrive("p", a, rot_in.at[a])

        def one(pz, carry):
            rows = pl.ds(pl.multiple_of(pz * 128 + a * RC, RC), RC)
            part = pl.ds(pl.multiple_of(pz * RC, RC), RC)
            for b in range(2):
                rot = None
                for px in range(4):
                    start = pl.multiple_of((b * 4 + pz) * RC, RC)
                    term = unpack_rows(rot_in.at[a, px], start, RC, 8 * RC)
                    rot = term if rot is None else rot + term
                at = pl.ds(b * 128, 128)
                moved_first = 0.9 * first[rows, at] + 0.1 * rot
                moved_second = 0.95 * second[rows, at] + 0.05 * rot * rot
                new_first[rows, at] = moved_first
                new_second[rows, at] = moved_second
                d_block[part, at] = (
                    moved_first / (1.0 - 0.9**STEP) / (jnp.sqrt(moved_second / (1.0 - 0.95**STEP)) + 1e-08)
                )
            return carry

        lax.fori_loop(0, 4, one, 0)
        pack(lambda b: d_block[:, pl.ds(b * 128, 128)], d_out.at[a], 4 * RC, 2)
        if a == NC - 1:
            for i, (src, dst) in enumerate(((new_first, first_out), (new_second, second_out))):
                store = pltpu.make_async_copy(src, dst, ls.at[2 + i])
                store.start()
                pending.append(store.wait)
        slot = xl * 2 + core
        for i in (2, 1, 3, 0):
            args = ("d", a, d_out.at[a], d_in.at[a, slot], (turn(x, i), y, z, xh))
            if i:
                send(*args)
            else:
                send_unless(xh == core, *args)

    def back(a):
        arrive("d", a, d_in.at[a])
        for j in range(4):
            for b in range(2):
                hi, lo = halves(unpack(d_in.at[a, j], b, 4 * RC, 2))
                at = pl.ds(j * 256 + b * 128, 128)
                d_parts[pl.ds(0, 4 * RC), at] = hi
                d_parts[pl.ds(4 * RC, 4 * RC), at] = lo

        both = dot_t(d_parts[...], right_hi[...])
        low = dot_t(d_parts[pl.ds(0, 4 * RC), :], right_lo[...])
        y_block[...] = both[0 : 4 * RC] + both[4 * RC : 8 * RC] + low
        for o in (2, 1, 3, 0):
            pz = turn(z, o)
            rows = pl.ds(pl.multiple_of(pz * RC, RC), RC)
            message = y_out.at[a, o] if o else y_in.at[a, z]
            pack(lambda b, rows=rows: y_block[rows, pl.ds(b * 128, 128)], message, RC, 8)
            if o:
                send("y1", a, message, y_in.at[a, z], (x, y, pz, core))

    def back_sum(a):
        arrive("y1", a, y_in.at[a, pl.ds(0, 3)])

        def one(b, carry):
            v = None
            for pz in range(4):
                term = unpack_rows(y_in.at[a, pz], pl.multiple_of(b * RC, RC), RC, 8 * RC)
                v = term if v is None else v + term
            y_sum[:, pl.ds(pl.multiple_of(b * 128, 128), 128)] = v
            return carry

        lax.fori_loop(0, 8, one, 0)
        for oc, pc in ((1, other), (0, core)):
            here = y_gather.at[a, core * 4 + z]
            message = y_gather_out.at[a] if oc else here
            pack(
                lambda b, pc=pc: y_sum[:, pl.ds(pl.multiple_of(pc * 512 + b * 128, 128), 128)], message, RC, 4
            )
            for o in (2, 1, 3, 0):
                if o or oc:
                    send("y2", a, message, here, (x, y, turn(z, o), pc))

    def raised_take(a):
        arrive("y2", a, y_gather.at[a, pl.ds(0, 7)])

        def one(i, carry):
            rows = pl.ds(pl.multiple_of(i * RC, RC), RC)
            for b in range(4):
                hi, lo = halves(unpack(y_gather.at[a, i], b, RC, 4))
                y_hi[rows, pl.ds(b * 128, 128)] = hi
                y_lo[rows, pl.ds(b * 128, 128)] = lo
            return carry

        lax.fori_loop(0, 8, one, 0)

    def raised(a, py):
        both = dot(lf[a, py], y_hi[...])
        v = both[0:256] + both[256:512] + dot(lf[a, py, pl.ds(0, 256), :], y_lo[...])
        u_acc[py] = u_acc[py] + v if a else v

    def right_piece(py, pc):
        def one(px, carry):
            for b in range(2):
                hi, lo = halves(decode(right_in[py, pc, px, pl.ds(b * 128, 128), :], BOUND))
                rows = pl.ds(pl.multiple_of(py * 256 + (px // 2) * 128, 128), 128)
                at = pl.ds(pl.multiple_of((px % 2) * 512 + pc * 256 + b * 128, 128), 128)
                right_hi[rows, at] = hi
                right_lo[rows, at] = lo
            return carry

        lax.fori_loop(0, 4, one, 0)

    def basis_take():
        arrive("rg", 2, right_in.at[pl.ds(0, 2), core])
        for o in (1, 3, 2):
            piece = right_in.at[turn(y, 4 - o), core]
            send("rc", 0, piece, piece, (x, y, z, other))
        for o in (0, 1, 3, 2):
            right_piece(turn(y, 4 - o), core)
        arrive("rc", 0, right_in.at[:, other])
        for o in (0, 1, 3, 2):
            right_piece(turn(y, 4 - o), other)

    def step(stage, a):
        if stage == 0:
            if a >= EARLY:
                left_forward(a)
                if a + 2 < NC:
                    left_spread(a + 2)
                left_take(a)
            turned(a)
            if a == 0:
                ring_pass("rg", right_half)
        if stage == 1:
            if a >= EARLY:
                flip(a)
            turned_sum(a)
            if a == 0:
                basis_take()
        if stage == 2:
            rotate(a)
        if stage == 3:
            moments(a)
        if stage == 4:
            back(a)
        if stage == 5:
            back_sum(a)
        if stage == 6 and a < NC - 1:
            raised_take(a)

            def one(py, carry, a=a):
                raised(a, py)
                return carry

            lax.fori_loop(0, 4, one, 0)

    for _, _, stage, a in sorted((s + OFF * a, TIE * a, s, a) for s in range(7) for a in range(NC)):
        step(stage, a)

    raised_take(NC - 1)
    for py in range(4):
        raised(NC - 1, py)
    for c in range(CC):
        for o in (2, 1, 3, 0):
            py = turn(y, o)
            message = u_out.at[c, o] if o else u_in.at[c, y]
            pack(lambda b, py=py, c=c: u_acc[py, :, pl.ds((c * CB + b) * 128, 128)], message, 256, CB)
            if o:
                send("u1", c, message, u_in.at[c, y], (x, py, z, core))
    for c in range(CC):
        arrive("u1", c, u_in.at[c, pl.ds(0, 3)])
        for b in range(CB):
            v = None
            for py in range(4):
                term = unpack(u_in.at[c, py], b, 256, CB)
                v = term if v is None else v + term
            u_sum[:, pl.ds(b * 128, 128)] = v
        here = u_last_in.at[c, x * 2 + core]
        for px in range(4):
            for pc in range(2):
                rows = pl.ds(px * 64 + pc * 32, 32)
                pack(lambda b, rows=rows: u_sum[rows, pl.ds(b * 128, 128)], u_last_out.at[c, px, pc], 32, CB)
        for o in (2, 1, 3, 0):
            for oc, pc in both_cores(o):
                px = turn(x, o)
                send("u2", c, u_last_out.at[c, px, pc], here, (px, y, z, pc))
        own = pltpu.make_async_copy(u_last_out.at[c, x, core], here, ls.at[4 + c])
        own.start()
        pending.append(own.wait)

    sent("lz", left_mid.at[:, pl.ds(0, 3)])
    sent("ly", left_in.at[:, 0, 0, pl.ds(0, 3)])
    sent("lg", left_in.at[:, pl.ds(0, 3), 0])
    sent("lc", left_in.at[:, :, 0])
    sent("g1", grad_in.at[pl.ds(0, 224)])
    sent("g2", grad_in.at[pl.ds(0, 768)])
    sent("r1", right_in.at[0, 0, pl.ds(0, 3)])
    sent("rg", right_in.at[pl.ds(0, 3), 0])
    sent("rc", right_in.at[:, 0])
    sent("h1", h_in.at[:, pl.ds(0, 7)])
    sent("h2", h_gather.at[:, pl.ds(0, 3)])
    for name, like in (("p", rot_in), ("d", d_in)):
        pl.when(xh == core)(lambda name=name, like=like: sent(name, like.at[:, pl.ds(0, 3)]))
        pl.when(xh != core)(lambda name=name, like=like: sent(name, like))
    sent("y1", y_in.at[:, pl.ds(0, 3)])
    sent("y2", y_gather.at[:, pl.ds(0, 7)])
    sent("u1", u_in.at[:, pl.ds(0, 3)])
    for c in range(CC):
        arrive("u2", c, u_last_in.at[c, pl.ds(0, 7)])
    sent("u2", u_last_in.at[:, pl.ds(0, 7)])
    for wait in pending:
        wait()


def finish(coded, first, second, update, new_first, new_second):
    new_first[...] = first[...]
    new_second[...] = second[...]
    for c in range(CC):
        for px in range(4):
            for pc in range(2):
                for b in range(CB):
                    at = pl.ds(pc * 2048 + (c * CB + b) * 512 + px * 128, 128)
                    update[:, at] = unpack(coded.at[c, px * 2 + pc], b, 32, CB)


SEMAPHORES = (
    ("lz", NC), ("ly", NC), ("lg", NC), ("lc", NC), ("g1", 1), ("g2", 3), ("r1", 1), ("rg", 3), ("rc", 1),
    ("h1", NC), ("h2", NC), ("p", NC), ("d", NC), ("y1", NC), ("y2", NC), ("u1", CC), ("u2", CC),
)


def body(grad, left_basis, right_basis, first_moment, second_moment):
    vm = pltpu.VMEM
    count = sum(n for _, n in SEMAPHORES)
    scratch = [
        vm((NC, 4, 2 * RC, 128), BF16),
        vm((NC, 4, 2 * RC, 128), BF16),
        vm((NC, 4, 2, 4, 2 * RC, 128), BF16),
        vm((NC, 2, 8 * RC, 1024), BF16),
        vm((NC, 4, 512, 8 * RC), BF16),
        vm((4, 2, 32, 512), BF16),
        vm((1024, 512), BF16),
        vm((4, 256, 128), BF16),
        vm((4, 2, 4, 256, 128), BF16),
        vm((1024, 1024), BF16),
        vm((1024, 1024), BF16),
        vm((NC, 4, 2, 4 * RC + 16, 128), BF16),
        vm((NC, 8, 4 * RC + 16, 128), BF16),
        vm((NC, 4, 8 * RC + 16, 128), BF16),
        vm((RC, 1024), F32),
        vm((4 * RC, 512), F32),
        vm((8 * RC, 1024), BF16),
        vm((4 * RC, 1024), F32),
        vm((NC, 4, 8 * RC + 16, 128), BF16),
        vm((NC, 4, 8 * RC + 16, 128), BF16),
        vm((4 * RC, 256), F32),
        vm((NC, 8 * RC + 16, 128), BF16),
        vm((NC, 4, 8 * RC + 16, 128), BF16),
        vm((8 * RC, 1024), BF16),
        vm((4 * RC, 1024), F32),
        vm((RC, 1024), F32),
        vm((NC, 4, 8 * RC + 16, 128), BF16),
        vm((NC, 4, 8 * RC + 16, 128), BF16),
        vm((NC, 4 * RC + 16, 128), BF16),
        vm((NC, 8, 4 * RC + 16, 128), BF16),
        vm((8 * RC, 512), BF16),
        vm((8 * RC, 512), BF16),
        vm((4, 256, 512), F32),
        vm((256, 128 * CB), F32),
        vm((CC, 4, 256 * CB + 16, 128), BF16),
        vm((CC, 4, 256 * CB + 16, 128), BF16),
        vm((CC, 4, 2, 32 * CB + 16, 128), BF16),
        vm((512, 256), F32),
        vm((512, 256), F32),
        vm((512, 256), F32),
        vm((512, 256), F32),
        pltpu.SemaphoreType.DMA((len(SEMAPHORES),)),
        pltpu.SemaphoreType.DMA((count,)),
        pltpu.SemaphoreType.DMA((4 + CC,)),
    ]
    whole = pl.BlockSpec(memory_space=pltpu.VMEM)
    there = pl.BlockSpec(memory_space=pl.ANY)
    square = jax.ShapeDtypeStruct((512, 256), F32)
    coded, new_first, new_second = pl.pallas_call(
        kernel,
        out_shape=(jax.ShapeDtypeStruct((CC, 8, 32 * CB + 16, 128), BF16), square, square),
        in_specs=[whole, whole, whole, there, there],
        out_specs=(there,) * 3,
        scratch_shapes=scratch,
        compiler_params=pltpu.CompilerParams(
            collective_id=0, has_side_effects=True, vmem_limit_bytes=56 * 2**20
        ),
    )(grad, left_basis, right_basis, first_moment, second_moment)
    return pl.pallas_call(
        finish,
        out_shape=(jax.ShapeDtypeStruct((32, 4096), F32), square, square),
        in_specs=[whole] * 3,
        out_specs=(whole,) * 3,
    )(coded, new_first, new_second)


def solution(mesh):
    placed = (
        P(("dp", "tensor"), None),
        P("dp", "tensor"),
        P("dp", "tensor"),
        P("dp", "tensor"),
        P("dp", "tensor"),
    )
    return jax.shard_map(
        body,
        mesh=mesh,
        in_specs=placed,
        out_specs=(P(("dp", "tensor"), None), P("dp", "tensor"), P("dp", "tensor")),
        check_vma=False,
    )
```

time: 121 us -> 112 us (0.926)
  Pallas kernels: 120 us -> 112 us
    pallas_call x1, Pallas kernels: 118 us -> 109 us  [body(): pl.pallas_call(kernel, out_shape=(jax.ShapeDtypeStruct((CC, 8, 32 * CB +...]
where the time goes in v4:
time: 112 us
  Pallas kernels  112 us (100%)
    pallas_call x1, Pallas kernels, body(): pl.pallas_call(kernel, out_shape=(jax.ShapeDtypeStruct((CC, 8, 32 * CB +...  109 us
    pallas_call x1, Pallas kernels, body(): pl.pallas_call(finish, out_shape=(jax.ShapeDtypeStruct((32, 4096), F32),...  2.49 us

profile of v4, /device:TPU:1, one launch (start us, length us, event | category | flops | bytes accessed | tf_op | source)
XLA Modules:
  0.0 112.2 jit_solution(4138486429720044537)
XLA Ops:
  0.6 109.0 %shard_map.76 = (bf16[4,8,48,128]{3,2,1,0:T(8,128)(2,1)}, f32[512,256]{1,0:T(8,128)}, f32[512,256]{1,0:T(8,128)}) custom-call(bf16[32,4096]{1,0:T(8,128)(2,1)} %grad.1, f32[512,256]{1,0:T(8,128)} %left.1, f32[512,256]{1,0:T(8,128)} %right.1, f32[512,256]{1,0:T(8,128)} %first_hbm.1, f32[512,256]{1,0:T(8,128)} %second_hbm.1), custom_call_target="tpu_custom_call" | custom-call | tf_op jit(solution)/shard_map/pallas_call | solution.py:600
  109.7 2.5 %shard_map.77 = (f32[32,4096]{1,0:T(8,128)}, f32[512,256]{1,0:T(8,128)}, f32[512,256]{1,0:T(8,128)}) custom-call(bf16[4,8,48,128]{3,2,1,0:T(8,128)(2,1)} %get-tuple-element.6.coded, f32[512,256]{1,0:T(8,128)} %get-tuple-element.7.first, f32[512,256]{1,0:T(8,128)} %get-tuple-element.8.second), custom_call_target="tpu_custom_call" | custom-call | tf_op jit(solution)/shard_map/pallas_call | solution.py:610

commit v5 on v4

--- a/solution.py
+++ b/solution.py
@@ -68,10 +68,14 @@
 
 NC = 4
 RC = 128 // NC
-OFF = 1
-EARLY = 2
-TIE = -1
-CC = 4
+GRAD_FIRST = False
+ORDER = (
+    "turned0", "pass0", "turned1", "forward2", "take2", "turned2", "turned_sum0", "forward3", "take3", "turned_sum1",
+    "turned3", "basis0", "turned_sum2", "rotate0", "rotate1", "flip1", "turned_sum3", "moments0", "flip2", "rotate2",
+    "moments1", "rotate3", "back0", "back1", "moments2", "flip3", "back_sum0", "moments3", "back_sum1", "back2",
+    "back3", "raise0", "back_sum2", "raise1", "back_sum3", "raise2",
+)
+CC = 2
 CB = 4 // CC
 
 
@@ -79,7 +83,7 @@
     grad, left, right, first_hbm, second_hbm, u_last_in, first_out, second_out,
     left_out, left_mid, left_in, lt, lf, grad_out, grad_in, right_out, right_in, right_hi, right_lo,
     h_out, h_in, h_gather, h_part, h_block, h_parts, rot_block, rot_out, rot_in, d_block, d_out, d_in, d_parts,
-    y_block, y_sum, y_out, y_in, y_gather_out, y_gather, y_hi, y_lo, u_acc, u_sum, u_out, u_in, u_last_out,
+    y_block, y_sum, y_out, y_in, y_gather_out, y_gather, y_hi, y_lo, u_acc, u_sum, u_far_out, u_far_in, u_out, u_in, u_last_out,
     first, second, new_first, new_second, ss, rs, ls,
 ):
     dp = lax.axis_index("dp")
@@ -157,16 +161,6 @@
             px = turn(x, o)
             send("g1", 0, grad_out.at[px, pc], grad_in.at[own_rows], (px, y, z, pc))
     grad_in[own_rows] = grad_out[x, core]
-    for q in range(4):
-        for b in range(2):
-            right_out[q, pl.ds(b * 128, 128), :] = encode(
-                right[pl.ds(q * 128, 128), pl.ds(b * 128, 128)], 1.0 / BOUND
-            )
-    for o in (2, 1, 3):
-        px = turn(x, o)
-        send("r1", 0, right_out.at[px], right_in.at[y, core, x], (px, y, z, core))
-    right_in[y, core, x] = right_out[x]
-
     def ring_start(name, half):
         for up, h, part in ((1, 0, 0), (3, 1, 1), (1, 1, 2), (3, 0, 2)):
             send(name, part, half(y, h), half(y, h), (x, turn(y, up), z, core))
@@ -231,10 +225,24 @@
 
         lax.fori_loop(0, 8, one, 0)
 
-    for a in range(NC):
+    left_turn(0)
+    for q in range(4):
+        for b in range(2):
+            right_out[q, pl.ds(b * 128, 128), :] = encode(
+                right[pl.ds(q * 128, 128), pl.ds(b * 128, 128)], 1.0 / BOUND
+            )
+    right_in[y, core, x] = right_out[x]
+    if GRAD_FIRST:
+        arrive("g1", 0, grad_in.at[pl.ds(0, 224)])
+        ring_start("g2", grad_half)
+    for a in range(1, NC):
         left_turn(a)
-    arrive("g1", 0, grad_in.at[pl.ds(0, 224)])
-    ring_start("g2", grad_half)
+    if not GRAD_FIRST:
+        arrive("g1", 0, grad_in.at[pl.ds(0, 224)])
+        ring_start("g2", grad_half)
+    for o in (2, 1, 3):
+        px = turn(x, o)
+        send("r1", 0, right_out.at[px], right_in.at[y, core, x], (px, y, z, core))
     left_spread(0)
     left_spread(1)
     ring_pass("g2", grad_half)
@@ -245,12 +253,9 @@
     left_spread(2)
     left_take(0)
     flip(0)
-    for a in range(1, EARLY):
-        left_forward(a)
-        if a + 2 < NC:
-            left_spread(a + 2)
-        left_take(a)
-        flip(a)
+    left_forward(1)
+    left_spread(3)
+    left_take(1)
     arrive("g2", 2, grad_in.at[pl.ds(0, 512)])
 
     def turned(a):
@@ -437,60 +442,57 @@
         for o in (0, 1, 3, 2):
             right_piece(turn(y, 4 - o), other)
 
-    def step(stage, a):
-        if stage == 0:
-            if a >= EARLY:
-                left_forward(a)
-                if a + 2 < NC:
-                    left_spread(a + 2)
-                left_take(a)
-            turned(a)
-            if a == 0:
-                ring_pass("rg", right_half)
-        if stage == 1:
-            if a >= EARLY:
-                flip(a)
-            turned_sum(a)
-            if a == 0:
-                basis_take()
-        if stage == 2:
-            rotate(a)
-        if stage == 3:
-            moments(a)
-        if stage == 4:
-            back(a)
-        if stage == 5:
-            back_sum(a)
-        if stage == 6 and a < NC - 1:
-            raised_take(a)
-
-            def one(py, carry, a=a):
-                raised(a, py)
-                return carry
-
-            lax.fori_loop(0, 4, one, 0)
-
-    for _, _, stage, a in sorted((s + OFF * a, TIE * a, s, a) for s in range(7) for a in range(NC)):
-        step(stage, a)
+    def raise_all(a):
+        raised_take(a)
+
+        def one(py, carry):
+            raised(a, py)
+            return carry
+
+        lax.fori_loop(0, 4, one, 0)
+
+    steps = {
+        "turned": turned, "pass": lambda a: ring_pass("rg", right_half), "forward": left_forward, "take": left_take,
+        "turned_sum": turned_sum, "basis": lambda a: basis_take(), "rotate": rotate, "moments": moments, "flip": flip,
+        "back": back, "back_sum": back_sum, "raise": raise_all,
+    }
+    for name in ORDER:
+        steps[name[:-1]](int(name[-1]))
 
     raised_take(NC - 1)
-    for py in range(4):
-        raised(NC - 1, py)
+    def rows_of(py, h, c, b):
+        return u_acc[py, pl.ds(h * 128, 128), pl.ds((c * CB + b) * 128, 128)]
+
+    def to_neighbour(name, c, h, up, py, message, dst):
+        pack(lambda b: rows_of(py, h, c, b), message, 128, CB)
+        send(name, c, message, dst, (x, turn(y, up), z, core))
+
+    raised(NC - 1, turn(y, 2))
     for c in range(CC):
-        for o in (2, 1, 3, 0):
-            py = turn(y, o)
-            message = u_out.at[c, o] if o else u_in.at[c, y]
-            pack(lambda b, py=py, c=c: u_acc[py, :, pl.ds((c * CB + b) * 128, 128)], message, 256, CB)
-            if o:
-                send("u1", c, message, u_in.at[c, y], (x, py, z, core))
+        for h, up in ((0, 1), (1, 3)):
+            to_neighbour("uf", c, h, up, turn(y, 2), u_far_out.at[c, h], u_far_in.at[c, h])
+    raised(NC - 1, turn(y, 1))
+    raised(NC - 1, turn(y, 3))
     for c in range(CC):
-        arrive("u1", c, u_in.at[c, pl.ds(0, 3)])
+        for h, up, slot in ((1, 1, 0), (0, 3, 1)):
+            to_neighbour("u1", c, h, up, turn(y, up), u_out.at[c, slot, h], u_in.at[c, slot, h])
+    for c in range(CC):
+        arrive("uf", c, u_far_in.at[c])
+        for h, up, slot in ((0, 1, 0), (1, 3, 1)):
+            py = turn(y, up)
+            for b in range(CB):
+                at = pl.ds((c * CB + b) * 128, 128)
+                u_acc[py, pl.ds(h * 128, 128), at] += unpack(u_far_in.at[c, h], b, 128, CB)
+            to_neighbour("u1", c, h, up, py, u_out.at[c, slot, h], u_in.at[c, slot, h])
+    raised(NC - 1, y)
+    for c in range(CC):
+        arrive("u1", c, u_in.at[c])
         for b in range(CB):
-            v = None
-            for py in range(4):
-                term = unpack(u_in.at[c, py], b, 256, CB)
-                v = term if v is None else v + term
-            u_sum[:, pl.ds(b * 128, 128)] = v
+            for h in range(2):
+                v = rows_of(y, h, c, b)
+                for slot in range(2):
+                    v = v + unpack(u_in.at[c, slot, h], b, 128, CB)
+                u_sum[pl.ds(h * 128, 128), pl.ds(b * 128, 128)] = v
         here = u_last_in.at[c, x * 2 + core]
         for px in range(4):
             for pc in range(2):
@@ -520,7 +522,8 @@
         pl.when(xh != core)(lambda name=name, like=like: sent(name, like))
     sent("y1", y_in.at[:, pl.ds(0, 3)])
     sent("y2", y_gather.at[:, pl.ds(0, 7)])
-    sent("u1", u_in.at[:, pl.ds(0, 3)])
+    sent("uf", u_far_in)
+    sent("u1", u_in)
     for c in range(CC):
         arrive("u2", c, u_last_in.at[c, pl.ds(0, 7)])
     sent("u2", u_last_in.at[:, pl.ds(0, 7)])
@@ -541,7 +544,7 @@
 
 SEMAPHORES = (
     ("lz", NC), ("ly", NC), ("lg", NC), ("lc", NC), ("g1", 1), ("g2", 3), ("r1", 1), ("rg", 3), ("rc", 1),
-    ("h1", NC), ("h2", NC), ("p", NC), ("d", NC), ("y1", NC), ("y2", NC), ("u1", CC), ("u2", CC),
+    ("h1", NC), ("h2", NC), ("p", NC), ("d", NC), ("y1", NC), ("y2", NC), ("uf", CC), ("u1", CC), ("u2", CC),
 )
 
 
@@ -583,8 +586,10 @@
         vm((8 * RC, 512), BF16),
         vm((4, 256, 512), F32),
         vm((256, 128 * CB), F32),
-        vm((CC, 4, 256 * CB + 16, 128), BF16),
-        vm((CC, 4, 256 * CB + 16, 128), BF16),
+        vm((CC, 2, 128 * CB + 16, 128), BF16),
+        vm((CC, 2, 128 * CB + 16, 128), BF16),
+        vm((CC, 2, 2, 128 * CB + 16, 128), BF16),
+        vm((CC, 2, 2, 128 * CB + 16, 128), BF16),
         vm((CC, 4, 2, 32 * CB + 16, 128), BF16),
         vm((512, 256), F32),
         vm((512, 256), F32),

time: 112 us -> 107 us (0.955)
  Pallas kernels: 112 us -> 106 us
    pallas_call x1, Pallas kernels: 109 us -> 104 us  [body(): pl.pallas_call(kernel, out_shape=(jax.ShapeDtypeStruct((CC, 8, 32 * CB +...]
where the time goes in v5:
time: 107 us
  Pallas kernels  106 us (99%)
    pallas_call x1, Pallas kernels, body(): pl.pallas_call(kernel, out_shape=(jax.ShapeDtypeStruct((CC, 8, 32 * CB +...  104 us
    pallas_call x1, Pallas kernels, body(): pl.pallas_call(finish, out_shape=(jax.ShapeDtypeStruct((32, 4096), F32),...  2.47 us

profile of v5, /device:TPU:1, one launch (start us, length us, event | category | flops | bytes accessed | tf_op | source)
XLA Modules:
  0.0 106.9 jit_solution(10657721392294051158)
XLA Ops:
  0.6 103.8 %shard_map.76 = (bf16[2,8,80,128]{3,2,1,0:T(8,128)(2,1)}, f32[512,256]{1,0:T(8,128)}, f32[512,256]{1,0:T(8,128)}) custom-call(bf16[32,4096]{1,0:T(8,128)(2,1)} %grad.1, f32[512,256]{1,0:T(8,128)} %left.1, f32[512,256]{1,0:T(8,128)} %right.1, f32[512,256]{1,0:T(8,128)} %first_hbm.1, f32[512,256]{1,0:T(8,128)} %second_hbm.1), custom_call_target="tpu_custom_call" | custom-call | tf_op jit(solution)/shard_map/pallas_call | solution.py:605
  104.4 2.5 %shard_map.77 = (f32[32,4096]{1,0:T(8,128)}, f32[512,256]{1,0:T(8,128)}, f32[512,256]{1,0:T(8,128)}) custom-call(bf16[2,8,80,128]{3,2,1,0:T(8,128)(2,1)} %get-tuple-element.6.coded, f32[512,256]{1,0:T(8,128)} %get-tuple-element.7.first, f32[512,256]{1,0:T(8,128)} %get-tuple-element.8.second), custom_call_target="tpu_custom_call" | custom-call | tf_op jit(solution)/shard_map/pallas_call | solution.py:615

commit v6 on v5

--- a/solution.py
+++ b/solution.py
@@ -68,12 +68,13 @@
 
 NC = 4
 RC = 128 // NC
+RIGHT_LATE = True
 GRAD_FIRST = False
 ORDER = (
-    "turned0", "pass0", "turned1", "forward2", "take2", "turned2", "turned_sum0", "forward3", "take3", "turned_sum1",
-    "turned3", "basis0", "turned_sum2", "rotate0", "rotate1", "flip1", "turned_sum3", "moments0", "flip2", "rotate2",
-    "moments1", "rotate3", "back0", "back1", "moments2", "flip3", "back_sum0", "moments3", "back_sum1", "back2",
-    "back3", "raise0", "back_sum2", "raise1", "back_sum3", "raise2",
+    "turned0", "take1", "pass0", "turned1", "forward2", "take2", "turned_sum0", "forward3", "take3", "basis0",
+    "turned_sum1", "basis1", "turned2", "rotate0", "turned3", "rotate1", "turned_sum2", "moments0", "flip0",
+    "turned_sum3", "moments1", "flip1", "flip2", "rotate2", "back0", "rotate3", "back1", "moments2", "back_sum0",
+    "moments3", "back_sum1", "back2", "raise0", "back3", "raise1", "back_sum2", "flip3", "back_sum3", "raise2",
 )
 CC = 2
 CB = 4 // CC
@@ -247,15 +248,16 @@
     left_spread(1)
     ring_pass("g2", grad_half)
     arrive("r1", 0, right_in.at[0, 0, pl.ds(0, 3)])
-    ring_start("rg", right_half)
+    if not RIGHT_LATE:
+        ring_start("rg", right_half)
     send("rc", 0, right_in.at[y, core], right_in.at[y, core], (x, y, z, other))
     left_forward(0)
     left_spread(2)
     left_take(0)
-    flip(0)
+    if RIGHT_LATE:
+        ring_start("rg", right_half)
     left_forward(1)
     left_spread(3)
-    left_take(1)
     arrive("g2", 2, grad_in.at[pl.ds(0, 512)])
 
     def turned(a):
@@ -431,16 +433,18 @@
 
         lax.fori_loop(0, 4, one, 0)
 
-    def basis_take():
-        arrive("rg", 2, right_in.at[pl.ds(0, 2), core])
-        for o in (1, 3, 2):
-            piece = right_in.at[turn(y, 4 - o), core]
-            send("rc", 0, piece, piece, (x, y, z, other))
-        for o in (0, 1, 3, 2):
-            right_piece(turn(y, 4 - o), core)
-        arrive("rc", 0, right_in.at[:, other])
-        for o in (0, 1, 3, 2):
-            right_piece(turn(y, 4 - o), other)
+    def basis_take(part):
+        if part == 0:
+            arrive("rg", 2, right_in.at[pl.ds(0, 2), core])
+            for o in (1, 3, 2):
+                piece = right_in.at[turn(y, 4 - o), core]
+                send("rc", 0, piece, piece, (x, y, z, other))
+            for o in (0, 1, 3, 2):
+                right_piece(turn(y, 4 - o), core)
+        else:
+            arrive("rc", 0, right_in.at[:, other])
+            for o in (0, 1, 3, 2):
+                right_piece(turn(y, 4 - o), other)
 
     def raise_all(a):
         raised_take(a)
@@ -453,7 +457,7 @@
 
     steps = {
         "turned": turned, "pass": lambda a: ring_pass("rg", right_half), "forward": left_forward, "take": left_take,
-        "turned_sum": turned_sum, "basis": lambda a: basis_take(), "rotate": rotate, "moments": moments, "flip": flip,
+        "turned_sum": turned_sum, "basis": basis_take, "rotate": rotate, "moments": moments, "flip": flip,
         "back": back, "back_sum": back_sum, "raise": raise_all,
     }
     for name in ORDER:

time: 107 us -> 104 us (0.972)
  Pallas kernels: 106 us -> 103 us
    pallas_call x1, Pallas kernels: 104 us -> 101 us  [body(): pl.pallas_call(kernel, out_shape=(jax.ShapeDtypeStruct((CC, 8, 32 * CB +...]
where the time goes in v6:
time: 104 us
  Pallas kernels  103 us (99%)
    pallas_call x1, Pallas kernels, body(): pl.pallas_call(kernel, out_shape=(jax.ShapeDtypeStruct((CC, 8, 32 * CB +...  101 us
    pallas_call x1, Pallas kernels, body(): pl.pallas_call(finish, out_shape=(jax.ShapeDtypeStruct((32, 4096), F32),...  2.47 us

profile of v6, /device:TPU:1, one launch (start us, length us, event | category | flops | bytes accessed | tf_op | source)
XLA Modules:
  0.0 103.7 jit_solution(3443498555852993937)
XLA Ops:
  0.6 100.6 %shard_map.76 = (bf16[2,8,80,128]{3,2,1,0:T(8,128)(2,1)}, f32[512,256]{1,0:T(8,128)}, f32[512,256]{1,0:T(8,128)}) custom-call(bf16[32,4096]{1,0:T(8,128)(2,1)} %grad.1, f32[512,256]{1,0:T(8,128)} %left.1, f32[512,256]{1,0:T(8,128)} %right.1, f32[512,256]{1,0:T(8,128)} %first_hbm.1, f32[512,256]{1,0:T(8,128)} %second_hbm.1), custom_call_target="tpu_custom_call" | custom-call | tf_op jit(solution)/shard_map/pallas_call | solution.py:609
  101.2 2.5 %shard_map.77 = (f32[32,4096]{1,0:T(8,128)}, f32[512,256]{1,0:T(8,128)}, f32[512,256]{1,0:T(8,128)}) custom-call(bf16[2,8,80,128]{3,2,1,0:T(8,128)(2,1)} %get-tuple-element.6.coded, f32[512,256]{1,0:T(8,128)} %get-tuple-element.7.first, f32[512,256]{1,0:T(8,128)} %get-tuple-element.8.second), custom_call_target="tpu_custom_call" | custom-call | tf_op jit(solution)/shard_map/pallas_call | solution.py:619

commit v7 on v6

--- a/solution.py
+++ b/solution.py
@@ -71,10 +71,10 @@
 RIGHT_LATE = True
 GRAD_FIRST = False
 ORDER = (
-    "turned0", "take1", "pass0", "turned1", "forward2", "take2", "turned_sum0", "forward3", "take3", "basis0",
-    "turned_sum1", "basis1", "turned2", "rotate0", "turned3", "rotate1", "turned_sum2", "moments0", "flip0",
-    "turned_sum3", "moments1", "flip1", "flip2", "rotate2", "back0", "rotate3", "back1", "moments2", "back_sum0",
-    "moments3", "back_sum1", "back2", "raise0", "back3", "raise1", "back_sum2", "flip3", "back_sum3", "raise2",
+    "turned0", "take1", "turned1", "pass0", "forward2", "take2", "turned_sum0", "forward3", "take3", "turned_sum1",
+    "turned2", "basis0", "basis1", "rotate0", "turned3", "rotate1", "turned_sum2", "flip0", "moments0",
+    "turned_sum3", "flip1", "moments1", "rotate2", "back0", "rotate3", "back1", "moments2", "flip2", "back_sum0",
+    "flip3", "moments3", "back_sum1", "back2", "back3", "raise0", "back_sum2", "raise1", "back_sum3", "raise2",
 )
 CC = 2
 CB = 4 // CC

time: 104 us -> 103 us (level)
  no operation moved by 1% of the time
where the time goes in v7:
time: 103 us
  Pallas kernels  102 us (99%)
    pallas_call x1, Pallas kernels, body(): pl.pallas_call(kernel, out_shape=(jax.ShapeDtypeStruct((CC, 8, 32 * CB +...  99.9 us
    pallas_call x1, Pallas kernels, body(): pl.pallas_call(finish, out_shape=(jax.ShapeDtypeStruct((32, 4096), F32),...  2.47 us

profile of v7, /device:TPU:1, one launch (start us, length us, event | category | flops | bytes accessed | tf_op | source)
XLA Modules:
  0.0 103.1 jit_solution(6162410675421038321)
XLA Ops:
  0.6 99.9 %shard_map.76 = (bf16[2,8,80,128]{3,2,1,0:T(8,128)(2,1)}, f32[512,256]{1,0:T(8,128)}, f32[512,256]{1,0:T(8,128)}) custom-call(bf16[32,4096]{1,0:T(8,128)(2,1)} %grad.1, f32[512,256]{1,0:T(8,128)} %left.1, f32[512,256]{1,0:T(8,128)} %right.1, f32[512,256]{1,0:T(8,128)} %first_hbm.1, f32[512,256]{1,0:T(8,128)} %second_hbm.1), custom_call_target="tpu_custom_call" | custom-call | tf_op jit(solution)/shard_map/pallas_call | solution.py:609
  100.6 2.5 %shard_map.77 = (f32[32,4096]{1,0:T(8,128)}, f32[512,256]{1,0:T(8,128)}, f32[512,256]{1,0:T(8,128)}) custom-call(bf16[2,8,80,128]{3,2,1,0:T(8,128)(2,1)} %get-tuple-element.6.coded, f32[512,256]{1,0:T(8,128)} %get-tuple-element.7.first, f32[512,256]{1,0:T(8,128)} %get-tuple-element.8.second), custom_call_target="tpu_custom_call" | custom-call | tf_op jit(solution)/shard_map/pallas_call | solution.py:619

commit v8 on v7

--- a/solution.py
+++ b/solution.py
@@ -73,7 +73,7 @@
 ORDER = (
     "turned0", "take1", "turned1", "pass0", "forward2", "take2", "turned_sum0", "forward3", "take3", "turned_sum1",
     "turned2", "basis0", "basis1", "rotate0", "turned3", "rotate1", "turned_sum2", "flip0", "moments0",
-    "turned_sum3", "flip1", "moments1", "rotate2", "back0", "rotate3", "back1", "moments2", "flip2", "back_sum0",
+    "turned_sum3", "flip1", "moments1", "rotate2", "rotate3", "back0", "back1", "moments2", "flip2", "back_sum0",
     "flip3", "moments3", "back_sum1", "back2", "back3", "raise0", "back_sum2", "raise1", "back_sum3", "raise2",
 )
 CC = 2

time: 103 us -> 104 us (level)
  no operation moved by 1% of the time
where the time goes in v8:
time: 104 us
  Pallas kernels  103 us (99%)
    pallas_call x1, Pallas kernels, body(): pl.pallas_call(kernel, out_shape=(jax.ShapeDtypeStruct((CC, 8, 32 * CB +...  101 us
    pallas_call x1, Pallas kernels, body(): pl.pallas_call(finish, out_shape=(jax.ShapeDtypeStruct((32, 4096), F32),...  2.47 us

profile of v8, /device:TPU:1, one launch (start us, length us, event | category | flops | bytes accessed | tf_op | source)
XLA Modules:
  0.0 103.9 jit_solution(3525689288653991178)
XLA Ops:
  0.6 100.8 %shard_map.76 = (bf16[2,8,80,128]{3,2,1,0:T(8,128)(2,1)}, f32[512,256]{1,0:T(8,128)}, f32[512,256]{1,0:T(8,128)}) custom-call(bf16[32,4096]{1,0:T(8,128)(2,1)} %grad.1, f32[512,256]{1,0:T(8,128)} %left.1, f32[512,256]{1,0:T(8,128)} %right.1, f32[512,256]{1,0:T(8,128)} %first_hbm.1, f32[512,256]{1,0:T(8,128)} %second_hbm.1), custom_call_target="tpu_custom_call" | custom-call | tf_op jit(solution)/shard_map/pallas_call | solution.py:609
  101.5 2.5 %shard_map.77 = (f32[32,4096]{1,0:T(8,128)}, f32[512,256]{1,0:T(8,128)}, f32[512,256]{1,0:T(8,128)}) custom-call(bf16[2,8,80,128]{3,2,1,0:T(8,128)(2,1)} %get-tuple-element.6.coded, f32[512,256]{1,0:T(8,128)} %get-tuple-element.7.first, f32[512,256]{1,0:T(8,128)} %get-tuple-element.8.second), custom_call_target="tpu_custom_call" | custom-call | tf_op jit(solution)/shard_map/pallas_call | solution.py:619
